TPU v7x, 32 devices: a whole 2x2x4 slice. The times are simulated.
32 devices in a mesh: dp: 4 (over y, x), expert: 8 (over z, core).
Axes of the slice: x: 2, y: 2, z: 4, core: 2. Of those that a mesh axis runs over, the one named last changes fastest.
Arguments:
- tokens: bfloat16 [8192, 4096], P(('dp', 'expert')), may hold values from -6 to 6
- latent_down: bfloat16 [4096, 1024], P(('dp', 'expert')), may hold values from -0.09375 to 0.09375
- latent_up: bfloat16 [1024, 4096], P(('dp', 'expert')), may hold values from -0.1875 to 0.1875
- expert_gate: bfloat16 [32, 1024, 2048], P('expert', None, 'dp'), may hold values from -0.1875 to 0.1875
- expert_up: bfloat16 [32, 1024, 2048], P('expert', None, 'dp'), may hold values from -0.1875 to 0.1875
- expert_down: bfloat16 [32, 2048, 1024], P('expert', 'dp'), may hold values from -0.125 to 0.125
- chosen_experts: int32 [8192, 4], P(('dp', 'expert')), may hold values from 0 to 31, all different within a row
- combine_weights: float32 [8192, 4], P(('dp', 'expert')), may hold values from 0.1 to 0.6
- capacity: int32 [32], replicated, may hold values from 16 to 32, as said below
- fallback: int32 [32, 128], P(('dp', 'expert')), may hold values from 0 to 31, as said below
Outputs:
- mixed: bfloat16 [8192, 4096], P(('dp', 'expert'))
Inputs may be any that keep to these rules, and one draw needn't show every extreme that they name: capacity is at most 32, and equals 32 for some expert. fallback[b, o] // 4 equals o modulo 32 // 4. `chosen_experts`: the 4 experts of one token differ.
All inputs are finite; a program needn't handle non-finite values.
Results may differ from a plain program's by a relative error of at most 0.014.
Values may be sent and summed in bfloat16 or wider, within the bound.
A program may use at most 128 MiB of HBM per device.

v0:
```python
import jax
import jax.numpy as jnp
from jax import lax
from jax.sharding import PartitionSpec as P


def assign_slots(block_experts, capacity, local_experts, slot_cap, spill_peer, peer_count):
    flat_experts = block_experts.reshape(-1)
    expert_count = capacity.shape[0]
    onehot = (flat_experts[:, None] == jnp.arange(expert_count, dtype=jnp.int32)[None, :]).astype(
        jnp.int32
    )
    earlier = jnp.cumsum(onehot, axis=0) - onehot
    slot_rank = jnp.sum(earlier * onehot, axis=1)
    slot_limit = jnp.sum(onehot * capacity[None, :], axis=1)
    is_main = slot_rank < slot_limit
    overflow = jnp.where(is_main, 0, 1).astype(jnp.int32)
    spill_number = jnp.cumsum(overflow) - overflow
    rows_peer = local_experts * slot_cap + spill_peer
    main_slot = (
        flat_experts // local_experts * rows_peer
        + flat_experts % local_experts * slot_cap
        + slot_rank
    )
    spill_slot = (
        spill_number % peer_count * rows_peer
        + local_experts * slot_cap
        + spill_number // peer_count
    )
    outside = peer_count * rows_peer
    in_spill = spill_number < spill_peer * peer_count
    return jnp.where(is_main, main_slot, jnp.where(in_spill, spill_slot, outside))


def whole_output(rows, gate_weight, up_weight, down_weight, team_size):
    gate_value = jnp.dot(rows, gate_weight, preferred_element_type=jnp.float32)
    up_value = jnp.dot(rows, up_weight, preferred_element_type=jnp.float32)
    hidden = (jax.nn.silu(gate_value) * up_value).astype(jnp.bfloat16)
    block_units = down_weight.shape[0] // team_size
    running = jnp.zeros((rows.shape[0], down_weight.shape[1]), jnp.float32)
    for quarter in range(team_size):
        lower_unit = quarter * block_units
        part_sum = jnp.dot(
            hidden[:, lower_unit : lower_unit + block_units],
            down_weight[lower_unit : lower_unit + block_units],
            preferred_element_type=jnp.float32,
        )
        running = running + part_sum.astype(jnp.bfloat16).astype(jnp.float32)
    return running.astype(jnp.bfloat16)


def on_device(
    tokens,
    latent_down,
    latent_up,
    expert_gate,
    expert_up,
    expert_down,
    chosen_experts,
    combine_weights,
    capacity,
    fallback,
):
    tok_count = tokens.shape[0]
    latent_width = expert_gate.shape[1]
    local_experts = expert_gate.shape[0]
    top_count = chosen_experts.shape[1]
    peer_count = lax.axis_size("expert")
    team_size = lax.axis_size("dp")
    expert_count = capacity.shape[0]
    spill_peer = fallback.shape[1] // peer_count
    slot_cap = tok_count * top_count // expert_count
    main_width = local_experts * slot_cap
    rows_peer = main_width + spill_peer
    columns = tokens
    latent = jnp.dot(
        columns,
        lax.all_gather(latent_down, ("dp", "expert"), axis=0, tiled=True),
        preferred_element_type=jnp.float32,
    ).astype(jnp.bfloat16)
    slot_index = assign_slots(
        chosen_experts, capacity, local_experts, slot_cap, spill_peer, peer_count
    )
    source_rows = jnp.repeat(latent, top_count, axis=0)
    buffer = (
        jnp.zeros((peer_count * rows_peer, latent_width), jnp.bfloat16)
        .at[slot_index]
        .set(source_rows, mode="drop")
    )
    buffer = buffer.reshape(peer_count, rows_peer, latent_width)
    spill_owner = fallback.reshape(spill_peer, peer_count).T % local_experts
    expert_range = jnp.arange(local_experts, dtype=jnp.int32)
    gate_whole, up_whole = (
        lax.all_to_all(expert_gate, "dp", split_axis=0, concat_axis=2, tiled=True),
        lax.all_to_all(expert_up, "dp", split_axis=0, concat_axis=2, tiled=True),
    )
    down_whole = lax.all_to_all(expert_down, "dp", split_axis=0, concat_axis=1, tiled=True)
    main_part = jnp.transpose(
        buffer[:, :main_width].reshape(peer_count, local_experts, slot_cap, latent_width),
        (1, 0, 2, 3),
    )
    spill_part = buffer[:, main_width:]
    owned = spill_owner[None, :, :, None] == expert_range[:, None, None, None]
    spill_masked = jnp.where(owned, spill_part[None], jnp.zeros_like(spill_part)[None])
    outgoing = jnp.concatenate([main_part, spill_masked], axis=2)
    slot_width = slot_cap + spill_peer
    outgoing = outgoing.reshape(local_experts * peer_count, slot_width, latent_width)
    arrived = lax.all_to_all(outgoing, ("dp", "expert"), split_axis=0, concat_axis=0, tiled=True)
    served = whole_output(
        arrived.reshape(-1, latent_width), gate_whole[0], up_whole[0], down_whole[0], team_size
    )
    served = served.reshape(local_experts * peer_count, slot_width, latent_width)
    back = lax.all_to_all(served, ("dp", "expert"), split_axis=0, concat_axis=0, tiled=True)
    back = back.reshape(local_experts, peer_count, slot_width, latent_width)
    main_back = jnp.transpose(back[:, :, :slot_cap], (1, 0, 2, 3)).reshape(
        peer_count, main_width, latent_width
    )
    spill_back = jnp.sum(back[:, :, slot_cap:].astype(jnp.float32), axis=0).astype(jnp.bfloat16)
    returned = jnp.concatenate([main_back, spill_back], axis=1)
    picked = jnp.take(
        returned.reshape(peer_count * rows_peer, latent_width),
        slot_index,
        axis=0,
        mode="fill",
        fill_value=0,
    )
    weighted = (
        picked.reshape(tok_count, top_count, latent_width).astype(jnp.float32)
        * combine_weights[:, :, None]
    )
    combined = jnp.sum(weighted, axis=1).astype(jnp.bfloat16)
    columns = combined
    result = jnp.dot(
        columns,
        lax.all_gather(latent_up, ("dp", "expert"), axis=0, tiled=True),
        preferred_element_type=jnp.float32,
    )
    return result.astype(jnp.bfloat16)


def solution(mesh):
    return jax.shard_map(
        on_device,
        mesh=mesh,
        in_specs=(
            P(("dp", "expert"), None),
            P(("dp", "expert"), None),
            P(("dp", "expert"), None),
            P("expert", None, "dp"),
            P("expert", None, "dp"),
            P("expert", "dp", None),
            P(("dp", "expert"), None),
            P(("dp", "expert"), None),
            P(),
            P(("dp", "expert"), None),
        ),
        out_specs=P(("dp", "expert"), None),
        check_vma=False,
    )
```

profile of v0, /device:TPU:0, one launch (start us, length us, event | category | flops | bytes accessed | tf_op | source)
XLA Modules:
  0.0 459.9 jit_solution(4119159005091661608)
XLA Ops:
  6.5 0.7 all-gather.3.cloned.1.call-update
  7.3 6.4 %copy.63 = bf16[4,1024,512]{1,2,0:T(8,128)(2,1)} copy(bf16[4,1024,512]{2,1,0:T(8,128)(2,1)} %param.13) | data formatting | bytes 8388608 | tf_op args[3]
  13.6 5.3 %all-to-all-start.1 = ((bf16[4,1024,512]{1,2,0:T(8,128)(2,1)}), bf16[4,1024,512]{1,2,0:T(8,128)(2,1)}, u32[]{:S(2)}, u32[]{:S(2)}) async-start(bf16[4,1024,512]{1,2,0:T(8,128)(2,1)} %copy.63), calls=%async_computation.1 | async-start | bytes 8388608 | tf_op jit(solution)/shard_map/all_to_all | solution.py:94
  18.9 0.1 copy.51
  19.3 0.1 reshape.356
  19.5 9.0 %reduce-window.15 = s32[32,8,128]{2,1,0:T(8,128)S(1)} reduce-window(s32[32,8,128]{2,1,0:T(8,128)S(1)} %fusion.10, s32[]{:T(128)} %constant.85.clone.1), window={size=1x1x128 pad=0_0x0_0x127_0}, to_apply=%region_0.0 | reduce-window | flops 4161536 | bytes 262148 | tf_op jit(solution)/shard_map/reduce-window
  28.6 0.1 copy.53
  29.1 0.3 reduce-window.19
  29.4 0.5 broadcast.437
  30.0 0.7 reduce.6
  31.1 87.7 %all-gather.3.cloned.1.call-done = bf16[4096,1024]{1,0:T(8,128)(2,1)} async-done(((bf16[128,1024]{1,0:T(8,128)(2,1)}), bf16[4096,1024]{1,0:T(8,128)(2,1)}) %all-gather.3.cloned.1.call-update) | async-done | bytes 8388624 | tf_op jit(solution)/shard_map/all_gather | solution.py:78
  118.7 5.7 %convolution_convert_fusion.5 = bf16[256,1024]{1,0:T(8,128)(2,1)S(1)} fusion(bf16[256,4096]{1,0:T(8,128)(2,1)S(1)} %copy-done, bf16[4096,1024]{1,0:T(8,128)(2,1)} %all-gather.3.cloned.1.call-done), kind=kOutput, calls=%fused_computation.17 | convolution fusion | flops 2147745792 | bytes 11010048 | tf_op jit(solution)/shard_map/dot_general | solution.py:76
  124.5 0.6 broadcast_in_dim.61
  125.1 2.0 reshape.379
  127.1 6.7 %scatter_custom_fusion = bf16[1152,1024]{1,0:T(8,128)(2,1)S(1)} fusion(s32[1024]{0:T(1024)S(1)} %bitcast.84, bf16[1024,1024]{1,0:T(8,128)(2,1)} %reshape.379, bf16[]{:T(256)} %constant.98.clone.1), kind=kCustom, calls=%fused_computation.18 | custom fusion | bytes 2359808 | tf_op jit(solution)/shard_map/scatter | solution.py:88
  133.8 0.2 slice.87
  134.0 0.1 broadcast_select_fusion
  134.2 0.5 pad_maximum_fusion
  134.7 2.1 copy.62
  136.7 3.2 all-to-all-start
  139.9 6.3 %copy.64 = bf16[4,1024,512]{1,2,0:T(8,128)(2,1)} copy(bf16[4,1024,512]{2,1,0:T(8,128)(2,1)} %param.14) | data formatting | bytes 8388608 | tf_op args[4]
  146.2 66.4 %all-to-all-done = bf16[32,48,1024]{2,1,0:T(8,128)(2,1)S(1)} async-done(((bf16[32,48,1024]{2,1,0:T(8,128)(2,1)}), bf16[32,48,1024]{2,1,0:T(8,128)(2,1)S(1)}, u32[]{:S(2)}, u32[]{:S(2)}) %all-to-all-start) | async-done | bytes 3145760 | tf_op jit(solution)/shard_map/all_to_all | solution.py:108
  212.5 4.8 %all-to-all-start.2 = ((bf16[4,1024,512]{1,2,0:T(8,128)(2,1)}), bf16[4,1024,512]{1,2,0:T(8,128)(2,1)}, u32[]{:S(2)}, u32[]{:S(2)}) async-start(bf16[4,1024,512]{1,2,0:T(8,128)(2,1)} %copy.64), calls=%async_computation.2 | async-start | bytes 8388608 | tf_op jit(solution)/shard_map/all_to_all | solution.py:95
  217.4 0.7 all-gather.5.cloned.1.call-update
  218.1 11.3 %fusion.32 = f32[1536,2048]{1,0:T(8,128)} fusion(bf16[1536,1024]{1,0:T(8,128)(2,1)S(1)} %bitcast.77, bf16[1024,2048]{0,1:T(8,128)(2,1)} %bitcast.15), kind=kOutput, calls=%fused_computation.92 | convolution fusion | flops 6442450944 | bytes 19922944 | tf_op jit(solution)/shard_map/dot_general | solution.py:36
  229.5 44.8 %all-to-all-done.2 = bf16[4,1024,512]{1,2,0:T(8,128)(2,1)} async-done(((bf16[4,1024,512]{1,2,0:T(8,128)(2,1)}), bf16[4,1024,512]{1,2,0:T(8,128)(2,1)}, u32[]{:S(2)}, u32[]{:S(2)}) %all-to-all-start.2) | async-done | bytes 4194336 | tf_op jit(solution)/shard_map/all_to_all | solution.py:95
  274.2 5.0 %all-to-all-start.3 = ((bf16[4,512,1024]{2,1,0:T(8,128)(2,1)}), bf16[4,512,1024]{2,1,0:T(8,128)(2,1)}, u32[]{:S(2)}, u32[]{:S(2)}) async-start(bf16[4,512,1024]{2,1,0:T(8,128)(2,1)} %param.15), calls=%async_computation.3 | async-start | bytes 8388608 | tf_op jit(solution)/shard_map/all_to_all | solution.py:97
  279.3 13.4 %multiply_convert_fusion = bf16[1536,2048]{1,0:T(8,128)(2,1)} fusion(f32[1536,2048]{1,0:T(8,128)} %fusion.32, bf16[1536,1024]{1,0:T(8,128)(2,1)S(1)} %bitcast.78, bf16[1024,2048]{0,1:T(8,128)(2,1)} %bitcast.18), kind=kOutput, calls=%fused_computation.2 | convolution fusion | flops 6461325312 | bytes 26214400 | tf_op jit(solution)/shard_map/dot_general | solution.py:37
  292.6 46.5 %all-to-all-done.3 = bf16[4,512,1024]{2,1,0:T(8,128)(2,1)} async-done(((bf16[4,512,1024]{2,1,0:T(8,128)(2,1)}), bf16[4,512,1024]{2,1,0:T(8,128)(2,1)}, u32[]{:S(2)}, u32[]{:S(2)}) %all-to-all-start.3) | async-done | bytes 4194336 | tf_op jit(solution)/shard_map/all_to_all | solution.py:97
  339.2 3.7 convolution_convert_fusion.1
  342.8 3.0 convolution_convert_fusion.2
  345.9 3.0 convolution_convert_fusion.3
  348.9 5.4 %add_convert_fusion = bf16[1536,1024]{1,0:T(8,128)(2,1)} fusion(bf16[1536,1024]{1,0:T(8,128)(2,1)S(1)} %convolution_convert_fusion.1, bf16[1536,1024]{1,0:T(8,128)(2,1)S(1)} %convolution_convert_fusion.2, bf16[1536,1024]{1,0:T(8,128)(2,1)S(1)} %convolution_convert_fusion.3, bf16[1536,2048]{1,0:T(8,128)(2,1)S(1)} %copy-done.5, ...), kind=kOutput, calls=%fused_computation.3 | convolution fusion | flops 1624768512 | bytes 15204352 | tf_op jit(solution)/shard_map/dot_general | solution.py:43
  354.4 3.0 all-to-all-start.4
  357.4 0.1 reshape.353
  357.5 0.1 reduce_sum.48
  357.7 0.1 reduce_sum.50
  358.2 0.2 copy.59
  358.4 0.8 copy.66
  359.3 70.5 %all-to-all-done.4 = bf16[32,48,1024]{2,1,0:T(8,128)(2,1)S(1)} async-done(((bf16[32,48,1024]{2,1,0:T(8,128)(2,1)}), bf16[32,48,1024]{2,1,0:T(8,128)(2,1)S(1)}, u32[]{:S(2)}, u32[]{:S(2)}) %all-to-all-start.4) | async-done | bytes 3145760 | tf_op jit(solution)/shard_map/all_to_all | solution.py:113
  429.8 0.2 slice_bitcast_fusion
  430.0 0.2 copy.65
  430.2 0.2 slice_reduce_fusion
  430.3 0.3 pad_maximum_fusion.1
  430.7 5.3 %gather_fusion = bf16[1024,1024]{1,0:T(8,128)(2,1)} fusion(bf16[1152,1024]{1,0:T(8,128)(2,1)S(1)} %bitcast.70, s32[1024]{0:T(1024)S(1)} %broadcast_clamp_fusion), kind=kCustom, calls=%fused_computation | custom fusion | bytes 4198400 | tf_op jit(solution)/shard_map/jit(_take)/gather | solution.py:120
  436.0 4.1 gather.7
  440.1 5.9 %multiply_reduce_fusion = bf16[256,1024]{1,0:T(8,128)(2,1)S(1)} fusion(f32[256,4]{1,0:T(8,128)S(1)} %copy.66, bf16[256,4,1024]{2,1,0:T(4,128)(2,1)} %gather.7, pred[256,4]{1,0:T(8,128)(4,1)S(1)} %copy.59), kind=kLoop, calls=%fused_computation.5 | loop fusion | flops 3932160 | bytes 2626560 | tf_op jit(solution)/shard_map/reduce_sum | solution.py:131
  446.0 7.0 %convolution_convert_fusion = bf16[256,4096]{1,0:T(8,128)(2,1)} fusion(bf16[1024,4096]{1,0:T(8,128)(2,1)} %all-gather.5.cloned.1.call-done, bf16[256,1024]{1,0:T(8,128)(2,1)S(1)} %multiply_reduce_fusion), kind=kOutput, calls=%fused_computation.4 | convolution fusion | flops 2148532224 | bytes 11010048 | tf_op jit(solution)/shard_map/dot_general | solution.py:133
  (43 shorter events, 1.7 us)
Async XLA Ops:
  6.5 112.2 %copy-start = (bf16[256,4096]{1,0:T(8,128)(2,1)S(1)}, bf16[256,4096]{1,0:T(8,128)(2,1)}, u32[]{:S(2)}) copy-start(bf16[256,4096]{1,0:T(8,128)(2,1)} %param.10) | copy-start | bytes 6291460
  6.5 112.2 %all-gather.3.cloned.1.call-start = ((), (), s32[]{:S(2)}) async-start(), calls=%async_computation.5 | async-start | bytes 8650752 | tf_op jit(solution)/shard_map/all_gather | solution.py:78
  13.6 5.3 %copy-start.2 = (s32[256,4]{0,1:T(4,128)S(1)}, s32[256,4]{0,1:T(4,128)}, u32[]{:S(2)}) copy-start(s32[256,4]{0,1:T(4,128)} %param.16) | copy-start | bytes 12292
  13.6 15.3 %copy-start.3 = (s32[32]{0:T(128)S(1)}, s32[32]{0:T(128)}, u32[]{:S(2)}) copy-start(s32[32]{0:T(128)} %param.18) | copy-start | bytes 388
  13.6 16.3 %copy-start.4 = (s32[1,128]{1,0:T(1,128)S(1)}, s32[1,128]{1,0:T(1,128)}, u32[]{:S(2)}) copy-start(s32[1,128]{1,0:T(1,128)} %param.19) | copy-start | bytes 1540
  13.6 123.1 %all-to-all-start.1 = ((bf16[4,1024,512]{1,2,0:T(8,128)(2,1)}), bf16[4,1024,512]{1,2,0:T(8,128)(2,1)}, u32[]{:S(2)}, u32[]{:S(2)}) async-start(bf16[4,1024,512]{1,2,0:T(8,128)(2,1)} %copy.63), calls=%async_computation.1 | async-start | bytes 8388608 | tf_op jit(solution)/shard_map/all_to_all | solution.py:94
  136.7 75.8 %all-to-all-start = ((bf16[32,48,1024]{2,1,0:T(8,128)(2,1)}), bf16[32,48,1024]{2,1,0:T(8,128)(2,1)S(1)}, u32[]{:S(2)}, u32[]{:S(2)}) async-start(bf16[32,48,1024]{2,1,0:T(8,128)(2,1)} %bitcast.11), calls=%async_computation | async-start | bytes 6291456 | tf_op jit(solution)/shard_map/all_to_all | solution.py:108
  212.5 61.7 %all-to-all-start.2 = ((bf16[4,1024,512]{1,2,0:T(8,128)(2,1)}), bf16[4,1024,512]{1,2,0:T(8,128)(2,1)}, u32[]{:S(2)}, u32[]{:S(2)}) async-start(bf16[4,1024,512]{1,2,0:T(8,128)(2,1)} %copy.64), calls=%async_computation.2 | async-start | bytes 8388608 | tf_op jit(solution)/shard_map/all_to_all | solution.py:95
  217.4 228.6 %all-gather.5.cloned.1.call-start = ((), (), s32[]{:S(2)}) async-start(), calls=%async_computation.6 | async-start | bytes 8650752 | tf_op jit(solution)/shard_map/all_gather | solution.py:135
  274.2 64.9 %all-to-all-start.3 = ((bf16[4,512,1024]{2,1,0:T(8,128)(2,1)}), bf16[4,512,1024]{2,1,0:T(8,128)(2,1)}, u32[]{:S(2)}, u32[]{:S(2)}) async-start(bf16[4,512,1024]{2,1,0:T(8,128)(2,1)} %param.15), calls=%async_computation.3 | async-start | bytes 8388608 | tf_op jit(solution)/shard_map/all_to_all | solution.py:97
  339.2 3.7 copy-start.5
  354.4 75.4 %all-to-all-start.4 = ((bf16[32,48,1024]{2,1,0:T(8,128)(2,1)}), bf16[32,48,1024]{2,1,0:T(8,128)(2,1)S(1)}, u32[]{:S(2)}, u32[]{:S(2)}) async-start(bf16[32,48,1024]{2,1,0:T(8,128)(2,1)} %bitcast.79), calls=%async_computation.4 | async-start | bytes 6291456 | tf_op jit(solution)/shard_map/all_to_all | solution.py:113
  440.1 12.9 %copy-start.1 = (bf16[256,4096]{1,0:T(8,128)(2,1)S(1)}, bf16[256,4096]{1,0:T(8,128)(2,1)}, u32[]{:S(2)}) copy-start(bf16[256,4096]{1,0:T(8,128)(2,1)} %param.10) | copy-start | bytes 6291460
Sparse Core Ops, SparseCore 0:
  10.4 108.3 all-gather.2
  221.2 119.9 all-gather.4
where the time goes:
time: 461 us; the launch traced here: 460 us
  waiting for transfers between devices  317 us (69%)
  matrix products  52.6 us (11%)
  local copies, waits for them, and re-layouts  37.5 us (8%)
  starting transfers between devices  21.4 us (5%)
  other arithmetic  17.4 us (4%)
  between operations  13.7 us (3%)
    all_gather x1, waiting for transfers between devices, on_device(): lax.all_gather(latent_down, ('dp', 'expert'), axis=0, tiled=True)  87.7 us
    all_to_all x1, waiting for transfers between devices, on_device(): lax.all_to_all(served, ('dp', 'expert'), split_axis=0, concat_axis=0, til...  70.5 us
    all_to_all x1, waiting for transfers between devices, on_device(): lax.all_to_all(outgoing, ('dp', 'expert'), split_axis=0, concat_axis=0, t...  66.4 us
    all_to_all x1, waiting for transfers between devices, on_device(): lax.all_to_all(expert_down, 'dp', split_axis=0, concat_axis=1, tiled=True)  46.5 us
    all_to_all x1, waiting for transfers between devices, on_device(): lax.all_to_all(expert_up, 'dp', split_axis=0, concat_axis=2, tiled=True)  44.8 us
    dot_general x4, matrix products, whole_output(): jnp.dot(hidden[:, lower_unit:lower_unit + block_units], down_weight[lower...  15.2 us
    unnamed x17, local copies, waits for them, and re-layouts  14.1 us
    dot_general x1, matrix products, whole_output(): up_value = jnp.dot(rows, up_weight, preferred_element_type=jnp.float32)  13.4 us
  transfers between devices with their start and end apart: 7, of which 5 were waited for; matrix products, arithmetic and copies ran while one was open for 22% of the time, Pallas kernels for 0%

commit v1 on v0

v1 whole, which is shorter than its diff:
```python
import jax
import jax.numpy as jnp
from jax import lax
from jax.sharding import Mesh
from jax.sharding import PartitionSpec as P

ALL = ("dp", "pair", "core")
PLANE = ("dp", "pair")


def dot32(a, b):
    return jnp.dot(a, b, preferred_element_type=jnp.float32)


def place_rows(block_experts, capacity, fallback, local_experts, slot_cap, spill_peer, peer_count):
    flat_experts = block_experts.reshape(-1)
    expert_count = capacity.shape[0]
    onehot = (flat_experts[:, None] == jnp.arange(expert_count, dtype=jnp.int32)[None, :]).astype(
        jnp.int32
    )
    earlier = jnp.cumsum(onehot, axis=0) - onehot
    slot_rank = jnp.sum(earlier * onehot, axis=1)
    slot_limit = jnp.sum(onehot * capacity[None, :], axis=1)
    is_main = slot_rank < slot_limit
    overflow = jnp.where(is_main, 0, 1).astype(jnp.int32)
    spill_number = jnp.cumsum(overflow) - overflow
    spill_all = spill_peer * peer_count
    in_spill = spill_number < spill_all
    number_hot = spill_number[:, None] == jnp.arange(spill_all, dtype=jnp.int32)[None, :]
    spill_target = jnp.sum(jnp.where(number_hot, fallback.reshape(1, -1), 0), axis=1)
    target = jnp.where(is_main, flat_experts, spill_target)
    slot = jnp.where(is_main, slot_rank, slot_cap + spill_number // peer_count)
    slot_width = slot_cap + spill_peer
    row = ((target % local_experts) * peer_count + target // local_experts) * slot_width + slot
    outside = local_experts * peer_count * slot_width
    return jnp.where(is_main | in_spill, row, outside).reshape(block_experts.shape)


def on_device(
    tokens,
    latent_down,
    latent_up,
    expert_gate,
    expert_up,
    expert_down,
    chosen_experts,
    combine_weights,
    capacity,
    fallback,
):
    tok_count = tokens.shape[0]
    latent_width = expert_gate.shape[1]
    local_experts = expert_gate.shape[0]
    top_count = chosen_experts.shape[1]
    peer_count = lax.axis_size("pair") * lax.axis_size("core")
    team_size = lax.axis_size("dp")
    expert_count = capacity.shape[0]
    spill_peer = fallback.shape[1] // peer_count
    slot_cap = tok_count * top_count // expert_count
    slot_width = slot_cap + spill_peer
    row_count = local_experts * peer_count * slot_width
    team = lax.axis_index("dp")
    core = lax.axis_index("core")

    def swap(value):
        return lax.ppermute(value, "core", [(0, 1), (1, 0)])

    def ordered(mine, other, axis):
        first = jnp.where(core == 0, mine, other)
        second = jnp.where(core == 0, other, mine)
        return jnp.concatenate([first, second], axis=axis)

    def column_half(shard):
        half = shard.shape[1] // 2
        mine = lax.dynamic_slice_in_dim(shard, core * half, half, 1)
        other = swap(lax.dynamic_slice_in_dim(shard, (1 - core) * half, half, 1))
        return lax.all_gather(ordered(mine, other, 0), PLANE, axis=0, tiled=True)

    down_half = column_half(latent_down)
    partner_tokens = swap(tokens)

    blocks = []
    for shift in range(team_size):
        partner = jnp.bitwise_xor(team, shift)
        gate, up, down = (
            lax.dynamic_index_in_dim(w, partner, 0, keepdims=False)
            for w in (expert_gate, expert_up, expert_down)
        )
        part = jnp.concatenate([jnp.concatenate([gate, up], axis=1), down], axis=0)
        if shift:
            part = lax.ppermute(part, "dp", [(d, d ^ shift) for d in range(team_size)])
        blocks.append(part)

    rows_of = place_rows(
        chosen_experts, capacity, fallback, local_experts, slot_cap, spill_peer, peer_count
    )
    hit = rows_of[:, :, None] == jnp.arange(row_count, dtype=jnp.int32)[None, None, :]
    spread = jnp.any(hit, axis=1).astype(jnp.bfloat16)
    weight = jnp.sum(jnp.where(hit, combine_weights[:, :, None], 0.0), axis=1)
    weight_high = weight.astype(jnp.bfloat16)
    weight_low = (weight - weight_high.astype(jnp.float32)).astype(jnp.bfloat16)

    for_partner = dot32(partner_tokens, down_half).astype(jnp.bfloat16)
    from_partner = swap(for_partner)
    for_me = dot32(tokens, down_half).astype(jnp.bfloat16)
    latent = ordered(for_me, from_partner, 1)
    outgoing = lax.dot_general(
        spread, latent, (((0,), (0,)), ((), ())), preferred_element_type=jnp.float32
    ).astype(jnp.bfloat16)
    outgoing = outgoing.reshape(local_experts * peer_count, slot_width, latent_width)
    outgoing, latent_up = lax.optimization_barrier((outgoing, latent_up))
    arrived = lax.all_to_all(outgoing, ALL, split_axis=0, concat_axis=0, tiled=True)
    rows = arrived.reshape(-1, latent_width)

    total = jnp.zeros((row_count, latent_width), jnp.float32)
    units = expert_down.shape[1]
    for part in blocks:
        both = dot32(rows, part[:latent_width])
        hidden = (jax.nn.silu(both[:, :units]) * both[:, units:]).astype(jnp.bfloat16)
        total = total + dot32(hidden, part[latent_width:]).astype(jnp.bfloat16).astype(jnp.float32)
    served = total.astype(jnp.bfloat16).reshape(local_experts * peer_count, slot_width, latent_width)
    back = lax.all_to_all(served, ALL, split_axis=0, concat_axis=0, tiled=True)
    back = back.reshape(row_count, latent_width)
    combined = (dot32(weight_high, back) + dot32(weight_low, back)).astype(jnp.bfloat16)

    up_half = column_half(latent_up)
    up_whole = ordered(up_half, swap(up_half), 1)
    return dot32(combined, up_whole).astype(jnp.bfloat16)


def solution(mesh):
    teams, peers = mesh.devices.shape
    split = Mesh(mesh.devices.reshape(teams, peers // 2, 2), ALL)
    experts = ("pair", "core")
    mapped = jax.shard_map(
        on_device,
        mesh=split,
        in_specs=(
            P(ALL, None),
            P(ALL, None),
            P(ALL, None),
            P(experts, None, "dp"),
            P(experts, None, "dp"),
            P(experts, "dp", None),
            P(ALL, None),
            P(ALL, None),
            P(),
            P(ALL, None),
        ),
        out_specs=P(ALL, None),
        check_vma=False,
    )
    return mapped
```

time: 461 us -> 419 us (0.909)
  local copies, waits for them, and re-layouts: 37.5 us -> 10.6 us
  waiting for transfers between devices: 317 us -> 293 us
  other arithmetic: 17.4 us -> 29 us
  starting transfers between devices: 21.4 us -> 12.4 us
  matrix products: 52.6 us -> 60.1 us
    all_to_all x5 -> x2, waiting for transfers between devices: 228 us -> 140 us  [the longest x1 70.4 us: on_device(): lax.all_to_all(outgoing, ALL, split_axis=0, concat_axis=0, tiled=True)]
    ppermute x0 -> x8, waiting for transfers between devices: none -> 87.3 us  [the longest x3 86.3 us: on_device(): part = lax.ppermute(part, 'dp', [(d, d ^ shift) for d in range(team_size)])]
    all_gather x2, waiting for transfers between devices: 87.7 us -> 65.4 us  [column_half(): return lax.all_gather(ordered(mine, other, 0), PLANE, axis=0, tiled=True)]
    all_to_all x5 -> x2, starting transfers between devices: 21.4 us -> 7.24 us  [the longest x1 3.71 us: on_device(): back = lax.all_to_all(served, ALL, split_axis=0, concat_axis=0, tiled=True)]
    unnamed x17 -> x13, local copies, waits for them, and re-layouts: 14.1 us -> 1.62 us
    gather x2 -> x0, local copies, waits for them, and re-layouts: 9.45 us -> none  [on_device(): jnp.take(returned.reshape(peer_count * rows_peer, latent_width), slot_ind...]
    dot_general x8 -> x13, matrix products: 52.6 us -> 60.1 us  [the longest x12 57.4 us: dot32(): return jnp.dot(a, b, preferred_element_type=jnp.float32)]
    select_n x4 -> x5, other arithmetic: 0.24 us -> 7.3 us  [the longest x3 7.05 us: ordered(): first = jnp.where(core == 0, mine, other)]
  transfers between devices with their start and end apart: 7 -> 12, of which waited for: 5 -> 6; matrix products, arithmetic and copies ran while one was open for 22% -> 17% of each run, Pallas kernels for 0% -> 0%
where the time goes in v1:
time: 419 us
  waiting for transfers between devices  293 us (70%)
  matrix products  60.1 us (14%)
  other arithmetic  29 us (7%)
  between operations  13.7 us (3%)
  starting transfers between devices  12.4 us (3%)
  local copies, waits for them, and re-layouts  10.6 us (3%)
    ppermute x3, waiting for transfers between devices, on_device(): part = lax.ppermute(part, 'dp', [(d, d ^ shift) for d in range(team_size)])  86.3 us
    all_to_all x1, waiting for transfers between devices, on_device(): lax.all_to_all(outgoing, ALL, split_axis=0, concat_axis=0, tiled=True)  70.4 us
    all_to_all x1, waiting for transfers between devices, on_device(): back = lax.all_to_all(served, ALL, split_axis=0, concat_axis=0, tiled=True)  70 us
    all_gather x2, waiting for transfers between devices, column_half(): return lax.all_gather(ordered(mine, other, 0), PLANE, axis=0, tiled=True)  65.4 us
    dot_general x12, matrix products, dot32(): return jnp.dot(a, b, preferred_element_type=jnp.float32)  57.4 us
    another operation x5, other arithmetic  9.45 us
  transfers between devices with their start and end apart: 12, of which 6 were waited for; matrix products, arithmetic and copies ran while one was open for 17% of the time, Pallas kernels for 0%

profile of v1, /device:TPU:0, one launch (start us, length us, event | category | flops | bytes accessed | tf_op | source)
XLA Modules:
  0.0 419.0 jit_solution(5207787222120588748)
XLA Ops:
  6.5 0.9 constant_dynamic-slice_fusion.1
  7.5 0.5 collective-permute-start
  8.0 1.0 collective-permute-done
  9.0 0.9 broadcast_select_fusion.7
  9.9 0.7 pad_maximum_fusion.3
  10.7 0.4 collective-permute-start.1
  11.1 0.8 copy.20
  12.2 9.0 %reduce-window.15 = s32[32,8,128]{2,1,0:T(8,128)S(1)} reduce-window(s32[32,8,128]{2,1,0:T(8,128)S(1)} %fusion.55, s32[]{:T(128)} %constant.94.clone.1), window={size=1x1x128 pad=0_0x0_0x127_0}, to_apply=%region_0.1 | reduce-window | flops 4161536 | bytes 262148 | tf_op jit(solution)/shard_map/reduce-window
  21.6 0.7 select_reduce_fusion.2
  22.4 0.3 reduce-window.19
  23.4 0.4 select_reduce_fusion.1
  24.1 65.4 %all-gather.3.cloned.1.call-done = bf16[4096,512]{1,0:T(8,128)(2,1)} async-done(((bf16[256,512]{1,0:T(8,128)(2,1)}), bf16[4096,512]{1,0:T(8,128)(2,1)}) %all-gather.3.cloned.1.call-update) | async-done | bytes 4194320 | tf_op jit(solution)/shard_map/all_gather | solution.py:77
  89.4 4.2 fusion.28
  93.7 0.3 fusion.46
  94.0 1.2 fusion.4
  95.3 3.5 broadcast_select_fusion.3
  98.8 2.7 convolution_convert_fusion
  101.5 3.5 all-to-all-start
  105.0 0.2 all-gather.5.cloned.1.call-start
  105.3 2.3 dynamic-slice_bitcast_fusion
  107.6 0.8 copy-done
  108.4 4.3 %dynamic-slice_bitcast_fusion.1 = (bf16[1024,512]{1,0:T(8,128)(2,1)S(1)}, bf16[1024,512]{1,0:T(8,128)(2,1)S(1)}, bf16[1024,512]{1,0:T(8,128)(2,1)}, bf16[1024,51...) fusion(bf16[4,1024,512]{2,1,0:T(8,128)(2,1)S(1)} %copy-done, ...), kind=kLoop, calls=%fused_computation.49 | loop fusion | bytes 16777232 | tf_op jit(solution)/shard_map/jit(dynamic_index_in_dim)/squeeze | solution.py:86
  112.7 2.0 pad_maximum_fusion
  114.7 1.6 collective-permute-start.3
  116.3 2.0 pad_maximum_fusion.1
  118.3 1.5 collective-permute-start.4
  119.9 2.1 pad_maximum_fusion.2
  122.0 0.4 collective-permute-start.5
  122.4 1.0 broadcast_select_fusion.5
  123.4 0.7 pad_maximum_fusion.4
  124.1 70.4 %all-to-all-done = bf16[32,48,1024]{2,1,0:T(8,128)(2,1)} async-done(((bf16[32,48,1024]{2,1,0:T(8,128)(2,1)}), bf16[32,48,1024]{2,1,0:T(8,128)(2,1)}, u32[]{:S(2)}, u32[]{:S(2)}) %all-to-all-start) | async-done | bytes 3145760 | tf_op jit(solution)/shard_map/all_to_all | solution.py:112
  194.6 6.0 %fusion.18 = f32[1536,1024]{1,0:T(8,128)S(1)} fusion(bf16[1536,1024]{1,0:T(8,128)(2,1)} %bitcast.8, bf16[1024,512]{1,0:T(8,128)(2,1)} %get-tuple-element.21, bf16[1024,512]{1,0:T(8,128)(2,1)} %get-tuple-element.33), kind=kOutput, calls=%fused_computation.33 | convolution fusion | flops 3225419776 | bytes 11534336 | tf_op jit(solution)/shard_map/dot_general | solution.py:12
  200.5 3.2 convolution_convert_fusion.4
  203.7 30.9 %collective-permute-done.3 = bf16[1536,1024]{1,0:T(8,128)(2,1)} collective-permute-done((bf16[1536,1024]{1,0:T(8,128)(2,1)}, bf16[1536,1024]{1,0:T(8,128)(2,1)}, u32[]{:S(2)}, u32[]{:S(2)}) %collective-permute-start.3) | collective-permute-done | bytes 3145760 | tf_op jit(solution)/shard_map/ppermute | solution.py:91
  234.6 6.0 %fusion.16 = f32[1536,1024]{1,0:T(8,128)S(1)} fusion(bf16[1536,1024]{1,0:T(8,128)(2,1)} %bitcast.8, bf16[1536,1024]{1,0:T(8,128)(2,1)} %collective-permute-done.3), kind=kOutput, calls=%fused_computation.31 | convolution fusion | flops 3221225472 | bytes 11534336 | tf_op jit(solution)/shard_map/dot_general | solution.py:12
  240.7 6.3 %fusion.14 = f32[1536,1024]{1,0:T(8,128)S(1)} fusion(bf16[1536,1024]{1,0:T(8,128)(2,1)} %bitcast.8, bf16[1536,1024]{1,0:T(8,128)(2,1)} %collective-permute-done.4), kind=kOutput, calls=%fused_computation.29 | convolution fusion | flops 3221225472 | bytes 11534336 | tf_op jit(solution)/shard_map/dot_general | solution.py:12
  247.0 55.4 %collective-permute-done.5 = bf16[1536,1024]{1,0:T(8,128)(2,1)S(1)} collective-permute-done((bf16[1536,1024]{1,0:T(8,128)(2,1)}, bf16[1536,1024]{1,0:T(8,128)(2,1)S(1)}, u32[]{:S(2)}, u32[]{:S(2)}) %collective-permute-start.5) | collective-permute-done | bytes 3145760 | tf_op jit(solution)/shard_map/ppermute | solution.py:91
  302.4 5.4 %fusion.12 = f32[1536,1024]{1,0:T(8,128)S(1)} fusion(bf16[1536,1024]{1,0:T(8,128)(2,1)} %bitcast.8, bf16[1536,1024]{1,0:T(8,128)(2,1)S(1)} %collective-permute-done.5), kind=kOutput, calls=%fused_computation.27 | convolution fusion | flops 3221225472 | bytes 11534336 | tf_op jit(solution)/shard_map/dot_general | solution.py:12
  307.8 3.2 convolution_convert_fusion.3
  311.0 3.2 convolution_convert_fusion.2
  314.2 3.8 add_convert_fusion
  318.0 3.7 all-to-all-start.1
  321.7 0.3 collective-permute-start.7
  322.1 2.2 select_reduce_fusion
  324.3 70.0 %all-to-all-done.1 = bf16[32,48,1024]{2,1,0:T(8,128)(2,1)S(1)} async-done(((bf16[32,48,1024]{2,1,0:T(8,128)(2,1)}), bf16[32,48,1024]{2,1,0:T(8,128)(2,1)S(1)}, u32[]{:S(2)}, u32[]{:S(2)}) %all-to-all-start.1) | async-done | bytes 3145760 | tf_op jit(solution)/shard_map/all_to_all | solution.py:122
  394.3 3.5 fusion.40
  397.9 5.1 %broadcast_select_fusion.1 = (bf16[1024,2048]{1,0:T(8,128)(2,1)}, bf16[1024,2048]{1,0:T(8,128)(2,1)}) fusion(bf16[1024,2048]{1,0:T(8,128)(2,1)S(1)} %copy-done.1, bf16[1024,2048]{1,0:T(8,128)(2,1)} %collective-permute-done.7, pred[]{:T(512)S(6)} %eq.77), kind=kLoop, calls=%fused_computation.10 | loop fusion | flops 4194304 | bytes 16777216 | tf_op jit(solution)/shard_map/jit(_where)/select_n | solution.py:69
  403.0 9.1 %fusion.5 = bf16[256,4096]{1,0:T(8,128)(2,1)} fusion(bf16[1024,2048]{1,0:T(8,128)(2,1)} %get-tuple-element.14, bf16[1024,2048]{1,0:T(8,128)(2,1)} %get-tuple-element.13, f32[256,1024]{1,0:T(8,128)} %fusion.40, bf16[1536,1024]{1,0:T(8,128)(2,1)S(1)} %bitcast.67, f32[256,1536]{1,0:T(8,128)} %select_reduce_fusion), kind=kOutput, calls=%fused_computation.8 | convolution fusion | flops 2972712960 | bytes 16252928 | tf_op jit(solution)/shard_map/dot_general | solution.py:12
  (44 shorter events, 2.0 us)
Async XLA Ops:
  6.5 16.9 %copy-start.4 = (s32[1,128]{1,0:T(1,128)S(1)}, s32[1,128]{1,0:T(1,128)}, u32[]{:S(2)}) copy-start(s32[1,128]{1,0:T(1,128)} %param.19) | copy-start | bytes 1540
  6.5 82.9 %all-gather.3.cloned.1.call-start = ((), (), s32[]{:S(2)}) async-start(), calls=%async_computation.2 | async-start | bytes 4456448 | tf_op jit(solution)/shard_map/all_gather | solution.py:77
  7.5 1.5 collective-permute-start
  10.7 13.4 %collective-permute-start.1 = (bf16[256,4096]{1,0:T(8,128)(2,1)}, bf16[256,4096]{1,0:T(8,128)(2,1)}, u32[]{:S(2)}, u32[]{:S(2)}) collective-permute-start(bf16[256,4096]{1,0:T(8,128)(2,1)} %param.10), channel_id=1, source_target_pairs={{0,1},{1,0},{2,3},{3,2},{4,5},{5,4},{6,7},{7,6},{8,9},{9,8},{10,11... | collective-permute-start | bytes 6291464 | tf_op jit(solution)/shard_map/ppermute | solution.py:66
  24.1 71.2 %copy-start.5 = (bf16[256,4096]{1,0:T(8,128)(2,1)S(1)}, bf16[256,4096]{1,0:T(8,128)(2,1)}, u32[]{:S(2)}) copy-start(bf16[256,4096]{1,0:T(8,128)(2,1)} %param.10) | copy-start | bytes 6291460
  93.6 1.6 collective-permute-start.2
  101.5 93.1 %all-to-all-start = ((bf16[32,48,1024]{2,1,0:T(8,128)(2,1)}), bf16[32,48,1024]{2,1,0:T(8,128)(2,1)}, u32[]{:S(2)}, u32[]{:S(2)}) async-start(bf16[32,48,1024]{2,1,0:T(8,128)(2,1)} %bitcast.7), calls=%async_computation | async-start | bytes 6291456 | tf_op jit(solution)/shard_map/all_to_all | solution.py:112
  105.0 216.7 %all-gather.5.cloned.1.call-start = ((), (), s32[]{:S(2)}) async-start(), calls=%async_computation.3 | async-start | bytes 4456448 | tf_op jit(solution)/shard_map/all_gather | solution.py:77
  105.3 3.1 copy-start
  114.7 119.9 %collective-permute-start.3 = (bf16[1536,1024]{1,0:T(8,128)(2,1)}, bf16[1536,1024]{1,0:T(8,128)(2,1)}, u32[]{:S(2)}, u32[]{:S(2)}) collective-permute-start(bf16[1536,1024]{1,0:T(8,128)(2,1)} %pad_maximum_fusion), channel_id=1, source_target_pairs={{0,8},{8,0},{16,24},{24,16},{1,9},{9,1},{17,25},{25,17},{2,10},{10... | collective-permute-start | bytes 9437192 | tf_op jit(solution)/shard_map/ppermute | solution.py:91
  116.3 3.5 copy-start.2
  118.3 122.4 %collective-permute-start.4 = (bf16[1536,1024]{1,0:T(8,128)(2,1)}, bf16[1536,1024]{1,0:T(8,128)(2,1)}, u32[]{:S(2)}, u32[]{:S(2)}) collective-permute-start(bf16[1536,1024]{1,0:T(8,128)(2,1)} %pad_maximum_fusion.1), channel_id=1, source_target_pairs={{0,16},{8,24},{16,0},{24,8},{1,17},{9,25},{17,1},{25,9},{2,18},{10... | collective-permute-start | bytes 9437192 | tf_op jit(solution)/shard_map/ppermute | solution.py:91
  119.8 2.6 collective-permute-start.6
  122.0 180.4 %collective-permute-start.5 = (bf16[1536,1024]{1,0:T(8,128)(2,1)}, bf16[1536,1024]{1,0:T(8,128)(2,1)S(1)}, u32[]{:S(2)}, u32[]{:S(2)}) collective-permute-start(bf16[1536,1024]{1,0:T(8,128)(2,1)} %pad_maximum_fusion.2), channel_id=1, source_target_pairs={{0,24},{8,16},{16,8},{24,0},{1,25},{9,17},{17,9},{25,1},{2,26},{10... | collective-permute-start | bytes 9437192 | tf_op jit(solution)/shard_map/ppermute | solution.py:91
  318.0 4.1 copy-start.3
  318.0 76.3 %all-to-all-start.1 = ((bf16[32,48,1024]{2,1,0:T(8,128)(2,1)}), bf16[32,48,1024]{2,1,0:T(8,128)(2,1)S(1)}, u32[]{:S(2)}, u32[]{:S(2)}) async-start(bf16[32,48,1024]{2,1,0:T(8,128)(2,1)} %bitcast.68), calls=%async_computation.1 | async-start | bytes 6291456 | tf_op jit(solution)/shard_map/all_to_all | solution.py:122
  321.7 76.1 %collective-permute-start.7 = (bf16[1024,2048]{1,0:T(8,128)(2,1)}, bf16[1024,2048]{1,0:T(8,128)(2,1)}, u32[]{:S(2)}, u32[]{:S(2)}) collective-permute-start(bf16[1024,2048]{1,0:T(8,128)(2,1)} %all-gather.5.cloned.1.call-done), channel_id=1, source_target_pairs={{0,1},{1,0},{2,3},{3,2},{4,5},{5,4},{6,7},{7,6},{8,9},{9,8},{10,11... | collective-permute-start | bytes 12582920 | tf_op jit(solution)/shard_map/ppermute | solution.py:66
  394.3 3.5 copy-start.1
Sparse Core Ops, SparseCore 0:
  10.8 78.6 all-gather.2
  124.2 112.2 all-gather.4

commit v2 on v1

--- a/solution.py
+++ b/solution.py
@@ -87,9 +87,17 @@
             for w in (expert_gate, expert_up, expert_down)
         )
         part = jnp.concatenate([jnp.concatenate([gate, up], axis=1), down], axis=0)
-        if shift:
-            part = lax.ppermute(part, "dp", [(d, d ^ shift) for d in range(team_size)])
         blocks.append(part)
+
+    def exchange(shift):
+        pairs = [(d, d ^ shift) for d in range(team_size)]
+        return lax.ppermute(blocks[shift], "dp", pairs)
+
+    early = range(1, team_size - 1)
+    tied = lax.optimization_barrier((down_half, blocks[-1], *[exchange(s) for s in early]))
+    down_half, blocks[-1] = tied[:2]
+    blocks[1:-1] = tied[2:]
+    blocks[-1] = exchange(team_size - 1)
 
     rows_of = place_rows(
         chosen_experts, capacity, fallback, local_experts, slot_cap, spill_peer, peer_count
@@ -108,8 +116,8 @@
         spread, latent, (((0,), (0,)), ((), ())), preferred_element_type=jnp.float32
     ).astype(jnp.bfloat16)
     outgoing = outgoing.reshape(local_experts * peer_count, slot_width, latent_width)
-    outgoing, latent_up = lax.optimization_barrier((outgoing, latent_up))
     arrived = lax.all_to_all(outgoing, ALL, split_axis=0, concat_axis=0, tiled=True)
+    arrived, latent_up = lax.optimization_barrier((arrived, latent_up))
     rows = arrived.reshape(-1, latent_width)
 
     total = jnp.zeros((row_count, latent_width), jnp.float32)
@@ -120,11 +128,12 @@
         total = total + dot32(hidden, part[latent_width:]).astype(jnp.bfloat16).astype(jnp.float32)
     served = total.astype(jnp.bfloat16).reshape(local_experts * peer_count, slot_width, latent_width)
     back = lax.all_to_all(served, ALL, split_axis=0, concat_axis=0, tiled=True)
+    up_half = column_half(latent_up)
+    up_whole = ordered(up_half, swap(up_half), 1)
+    back, up_whole = lax.optimization_barrier((back, up_whole))
     back = back.reshape(row_count, latent_width)
     combined = (dot32(weight_high, back) + dot32(weight_low, back)).astype(jnp.bfloat16)
 
-    up_half = column_half(latent_up)
-    up_whole = ordered(up_half, swap(up_half), 1)
     return dot32(combined, up_whole).astype(jnp.bfloat16)
 
 

time: 419 us -> 425 us (1.014)
  other arithmetic: 29 us -> 37.7 us
  waiting for transfers between devices: 293 us -> 287 us
    all_to_all x1, waiting for transfers between devices: 70 us -> 0.01 us  [on_device(): back = lax.all_to_all(served, ALL, split_axis=0, concat_axis=0, tiled=True)]
    ppermute x3, waiting for transfers between devices: 86.3 us -> 123 us  [exchange(): return lax.ppermute(blocks[shift], 'dp', pairs)]
    all_gather x2, waiting for transfers between devices: 65.4 us -> 83.9 us  [column_half(): return lax.all_gather(ordered(mine, other, 0), PLANE, axis=0, tiled=True)]
    concatenate x2 -> x3, other arithmetic: 1.47 us -> 9.23 us  [ordered(): return jnp.concatenate([first, second], axis=axis)]
    ppermute x5, waiting for transfers between devices: 1 us -> 7.59 us  [swap(): return lax.ppermute(value, 'core', [(0, 1), (1, 0)])]
  transfers between devices with their start and end apart: 12 -> 12, of which waited for: 6 -> 7; matrix products, arithmetic and copies ran while one was open for 17% -> 19% of each run, Pallas kernels for 0% -> 0%
where the time goes in v2:
time: 425 us
  waiting for transfers between devices  287 us (68%)
  matrix products  60.3 us (14%)
  other arithmetic  37.7 us (9%)
  starting transfers between devices  14.4 us (3%)
  between operations  13.7 us (3%)
  local copies, waits for them, and re-layouts  11.5 us (3%)
    ppermute x3, waiting for transfers between devices, exchange(): return lax.ppermute(blocks[shift], 'dp', pairs)  123 us
    all_gather x2, waiting for transfers between devices, column_half(): return lax.all_gather(ordered(mine, other, 0), PLANE, axis=0, tiled=True)  83.9 us
    all_to_all x1, waiting for transfers between devices, on_device(): lax.all_to_all(outgoing, ALL, split_axis=0, concat_axis=0, tiled=True)  72.4 us
    dot_general x12, matrix products, dot32(): return jnp.dot(a, b, preferred_element_type=jnp.float32)  57.6 us
    another operation x5, other arithmetic  9.44 us
    concatenate x3, other arithmetic, ordered(): return jnp.concatenate([first, second], axis=axis)  9.23 us
  transfers between devices with their start and end apart: 12, of which 7 were waited for; matrix products, arithmetic and copies ran while one was open for 19% of the time, Pallas kernels for 0%

profile of v2, /device:TPU:0, one launch (start us, length us, event | category | flops | bytes accessed | tf_op | source)
XLA Modules:
  0.0 424.9 jit_solution(3960285751366291102)
XLA Ops:
  6.5 0.9 constant_dynamic-slice_fusion.1
  7.5 0.5 collective-permute-start
  8.0 1.0 collective-permute-done
  9.0 0.9 broadcast_select_fusion.7
  9.9 0.7 pad_maximum_fusion.4
  10.7 2.3 dynamic-slice_bitcast_fusion.2
  13.0 0.8 copy-done
  13.8 4.5 %dynamic-slice_bitcast_fusion = (bf16[1024,512]{1,0:T(8,128)(2,1)}, bf16[1024,512]{1,0:T(8,128)(2,1)S(1)}, bf16[1024,512]{1,0:T(8,128)(2,1)S(1)}, bf16[1024,512]...) fusion(bf16[4,1024,512]{2,1,0:T(8,128)(2,1)S(1)} %copy-done, ...), kind=kLoop, calls=%fused_computation.46 | loop fusion | bytes 16777232 | tf_op jit(solution)/shard_map/jit(dynamic_index_in_dim)/squeeze | solution.py:86
  18.3 2.0 pad_maximum_fusion.2
  20.3 2.8 collective-permute-start.1
  23.1 2.0 pad_maximum_fusion.3
  25.1 1.5 collective-permute-start.2
  27.0 9.0 %reduce-window.15 = s32[32,8,128]{2,1,0:T(8,128)S(1)} reduce-window(s32[32,8,128]{2,1,0:T(8,128)S(1)} %fusion.48, s32[]{:T(128)} %constant.94.clone.1), window={size=1x1x128 pad=0_0x0_0x127_0}, to_apply=%region_0.1 | reduce-window | flops 4161536 | bytes 262148 | tf_op jit(solution)/shard_map/reduce-window
  36.8 0.5 select_bitcast_fusion
  37.3 0.3 reduce-window.19
  37.8 0.8 reduce_sum.45
  38.7 0.7 select_subtract_fusion.1
  39.4 1.0 select_reduce_fusion.1
  40.4 0.8 reduce_sum.47
  41.4 2.1 pad_maximum_fusion.1
  43.5 72.6 %collective-permute-done.1 = bf16[1536,1024]{1,0:T(8,128)(2,1)} collective-permute-done((bf16[1536,1024]{1,0:T(8,128)(2,1)}, bf16[1536,1024]{1,0:T(8,128)(2,1)}, u32[]{:S(2)}, u32[]{:S(2)}) %collective-permute-start.1) | collective-permute-done | bytes 3145760 | tf_op jit(solution)/shard_map/ppermute | solution.py:94
  116.1 4.2 fusion.21
  120.7 1.2 fusion
  122.0 4.2 broadcast_select_fusion.3
  126.1 2.7 convolution_convert_fusion.1
  128.8 5.2 %all-to-all-start = ((bf16[32,48,1024]{2,1,0:T(8,128)(2,1)}), bf16[32,48,1024]{2,1,0:T(8,128)(2,1)}, u32[]{:S(2)}, u32[]{:S(2)}) async-start(bf16[32,48,1024]{2,1,0:T(8,128)(2,1)} %bitcast.16), calls=%async_computation | async-start | bytes 6291456 | tf_op jit(solution)/shard_map/all_to_all | solution.py:119
  134.3 72.4 %all-to-all-done = bf16[32,48,1024]{2,1,0:T(8,128)(2,1)} async-done(((bf16[32,48,1024]{2,1,0:T(8,128)(2,1)}), bf16[32,48,1024]{2,1,0:T(8,128)(2,1)}, u32[]{:S(2)}, u32[]{:S(2)}) %all-to-all-start) | async-done | bytes 3145760 | tf_op jit(solution)/shard_map/all_to_all | solution.py:119
  206.8 1.5 collective-permute-done.6
  208.2 1.0 broadcast_select_fusion.5
  209.2 0.7 pad_maximum_fusion.5
  209.9 0.9 collective-permute-start.5
  210.9 6.0 %fusion.7 = f32[1536,1024]{1,0:T(8,128)S(1)} fusion(bf16[1536,1024]{1,0:T(8,128)(2,1)} %bitcast.17, bf16[1024,512]{1,0:T(8,128)(2,1)} %get-tuple-element.31, bf16[1024,512]{1,0:T(8,128)(2,1)} %get-tuple-element.47), kind=kOutput, calls=%fused_computation.26 | convolution fusion | flops 3225419776 | bytes 11534336 | tf_op jit(solution)/shard_map/dot_general | solution.py:12
  216.8 3.2 convolution_convert_fusion.5
  220.1 6.0 %fusion.11 = f32[1536,1024]{1,0:T(8,128)S(1)} fusion(bf16[1536,1024]{1,0:T(8,128)(2,1)} %bitcast.17, bf16[1536,1024]{1,0:T(8,128)(2,1)} %collective-permute-done.2), kind=kOutput, calls=%fused_computation.30 | convolution fusion | flops 3221225472 | bytes 11534336 | tf_op jit(solution)/shard_map/dot_general | solution.py:12
  226.1 6.1 %fusion.13 = f32[1536,1024]{1,0:T(8,128)S(1)} fusion(bf16[1536,1024]{1,0:T(8,128)(2,1)} %bitcast.17, bf16[1536,1024]{1,0:T(8,128)(2,1)} %collective-permute-done.1), kind=kOutput, calls=%fused_computation.32 | convolution fusion | flops 3221225472 | bytes 11534336 | tf_op jit(solution)/shard_map/dot_general | solution.py:12
  232.1 50.8 %collective-permute-done.5 = bf16[1536,1024]{1,0:T(8,128)(2,1)S(1)} collective-permute-done((bf16[1536,1024]{1,0:T(8,128)(2,1)S(1)}, bf16[1536,1024]{1,0:T(8,128)(2,1)S(1)}, u32[]{:S(2)}, u32[]{:S(2)}) %collective-permute-start.5) | collective-permute-done | bytes 3145760 | tf_op jit(solution)/shard_map/ppermute | solution.py:94
  282.9 5.5 %fusion.5 = f32[1536,1024]{1,0:T(8,128)S(1)} fusion(bf16[1536,1024]{1,0:T(8,128)(2,1)} %bitcast.17, bf16[1536,1024]{1,0:T(8,128)(2,1)S(1)} %collective-permute-done.5), kind=kOutput, calls=%fused_computation.24 | convolution fusion | flops 3221225472 | bytes 11534336 | tf_op jit(solution)/shard_map/dot_general | solution.py:12
  288.5 3.1 convolution_convert_fusion.3
  291.6 3.2 convolution_convert_fusion.4
  294.8 3.6 add_convert_fusion
  298.4 2.9 all-to-all-start.1
  301.4 83.9 %all-gather.5.cloned.1.call-done = bf16[1024,2048]{1,0:T(8,128)(2,1)} async-done(((bf16[64,2048]{1,0:T(8,128)(2,1)}), bf16[1024,2048]{1,0:T(8,128)(2,1)}) %all-gather.5.cloned.1.call-update) | async-done | bytes 4194320 | tf_op jit(solution)/shard_map/all_gather | solution.py:77
  385.3 2.2 select_reduce_fusion
  387.5 5.1 %collective-permute-done.7 = bf16[1024,2048]{1,0:T(8,128)(2,1)S(1)} collective-permute-done((bf16[1024,2048]{1,0:T(8,128)(2,1)}, bf16[1024,2048]{1,0:T(8,128)(2,1)S(1)}, u32[]{:S(2)}, u32[]{:S(2)}) %collective-permute-start.7) | collective-permute-done | bytes 4194336 | tf_op jit(solution)/shard_map/ppermute | solution.py:66
  392.7 5.1 %broadcast_select_fusion.1 = (bf16[1024,2048]{1,0:T(8,128)(2,1)}, bf16[1024,2048]{1,0:T(8,128)(2,1)}) fusion(bf16[1024,2048]{1,0:T(8,128)(2,1)} %all-gather.5.cloned.1.call-done, bf16[1024,2048]{1,0:T(8,128)(2,1)S(1)} %collective-permute-done.7, pred[]{:T(512)S(6)} %eq.77), kind=kLoop, calls=%fused_computation.7 | loop fusion | flops 4194304 | bytes 16777216 | tf_op jit(solution)/shard_map/jit(_where)/select_n | solution.py:69
  397.7 7.8 %pad_maximum_fusion = bf16[1024,4096]{1,0:T(8,128)(2,1)} fusion(bf16[1024,2048]{1,0:T(8,128)(2,1)} %get-tuple-element.26, bf16[1024,2048]{1,0:T(8,128)(2,1)} %get-tuple-element.25), kind=kLoop, calls=%fused_computation | loop fusion | flops 16777216 | bytes 16777216 | tf_op jit(solution)/shard_map/concatenate | solution.py:71
  405.5 3.4 fusion.33
  408.9 9.2 %convolution_convert_fusion = bf16[256,4096]{1,0:T(8,128)(2,1)} fusion(bf16[1024,4096]{1,0:T(8,128)(2,1)} %pad_maximum_fusion, f32[256,1024]{1,0:T(8,128)} %fusion.33, bf16[1536,1024]{1,0:T(8,128)(2,1)S(1)} %bitcast.68, f32[256,1536]{1,0:T(8,128)} %select_reduce_fusion), kind=kOutput, calls=%fused_computation.5 | convolution fusion | flops 2955935744 | bytes 16252928 | tf_op jit(solution)/shard_map/dot_general | solution.py:12
  (49 shorter events, 2.4 us)
Async XLA Ops:
  6.5 109.6 %all-gather.3.cloned.1.call-start = ((), (), s32[]{:S(2)}) async-start(), calls=%async_computation.2 | async-start | bytes 4456448 | tf_op jit(solution)/shard_map/all_gather | solution.py:77
  7.5 1.5 collective-permute-start
  10.7 3.1 copy-start
  20.3 95.8 %collective-permute-start.1 = (bf16[1536,1024]{1,0:T(8,128)(2,1)}, bf16[1536,1024]{1,0:T(8,128)(2,1)}, u32[]{:S(2)}, u32[]{:S(2)}) collective-permute-start(bf16[1536,1024]{1,0:T(8,128)(2,1)} %pad_maximum_fusion.2), channel_id=1, source_target_pairs={{0,8},{8,0},{16,24},{24,16},{1,9},{9,1},{17,25},{25,17},{2,10},{10... | collective-permute-start | bytes 9437192 | tf_op jit(solution)/shard_map/ppermute | solution.py:94
  23.1 3.5 copy-start.6
  23.1 13.4 %copy-start.7 = (s32[32]{0:T(128)S(1)}, s32[32]{0:T(128)}, u32[]{:S(2)}) copy-start(s32[32]{0:T(128)} %param.18) | copy-start | bytes 388
  25.1 91.0 %collective-permute-start.2 = (bf16[1536,1024]{1,0:T(8,128)(2,1)}, bf16[1536,1024]{1,0:T(8,128)(2,1)}, u32[]{:S(2)}, u32[]{:S(2)}) collective-permute-start(bf16[1536,1024]{1,0:T(8,128)(2,1)} %pad_maximum_fusion.3), channel_id=1, source_target_pairs={{0,16},{8,24},{16,0},{24,8},{1,17},{9,25},{17,1},{25,9},{2,18},{10... | collective-permute-start | bytes 9437192 | tf_op jit(solution)/shard_map/ppermute | solution.py:94
  26.6 89.5 %collective-permute-start.3 = (bf16[256,4096]{1,0:T(8,128)(2,1)}, bf16[256,4096]{1,0:T(8,128)(2,1)}, u32[]{:S(2)}, u32[]{:S(2)}) collective-permute-start(bf16[256,4096]{1,0:T(8,128)(2,1)} %param.10), channel_id=1, source_target_pairs={{0,1},{1,0},{2,3},{3,2},{4,5},{5,4},{6,7},{7,6},{8,9},{9,8},{10,11... | collective-permute-start | bytes 6291464 | tf_op jit(solution)/shard_map/ppermute | solution.py:66
  43.5 76.9 %copy-start.2 = (s32[256,4]{1,0:T(8,128)S(1)}, s32[256,4]{1,0:T(8,128)}, u32[]{:S(2)}) copy-start(s32[256,4]{1,0:T(8,128)} %reduce_sum.45) | copy-start | bytes 12292
  43.5 76.9 %copy-start.3 = (s32[256,4]{1,0:T(8,128)S(1)}, s32[256,4]{1,0:T(8,128)}, u32[]{:S(2)}) copy-start(s32[256,4]{1,0:T(8,128)} %reduce_sum.47) | copy-start | bytes 12292
  120.3 1.7 collective-permute-start.4
  128.8 77.8 %copy-start.4 = (bf16[32,4096]{1,0:T(8,128)(2,1)S(1)}, bf16[32,4096]{1,0:T(8,128)(2,1)}, u32[]{:S(2)}) copy-start(bf16[32,4096]{1,0:T(8,128)(2,1)} %param.12) | copy-start | bytes 786436
  128.8 81.1 %copy-start.1 = (bf16[1536,1024]{1,0:T(8,128)(2,1)S(1)}, bf16[1536,1024]{1,0:T(8,128)(2,1)}, u32[]{:S(2)}) copy-start(bf16[1536,1024]{1,0:T(8,128)(2,1)} %pad_maximum_fusion.1) | copy-start | bytes 9437188
  128.8 77.8 %all-to-all-start = ((bf16[32,48,1024]{2,1,0:T(8,128)(2,1)}), bf16[32,48,1024]{2,1,0:T(8,128)(2,1)}, u32[]{:S(2)}, u32[]{:S(2)}) async-start(bf16[32,48,1024]{2,1,0:T(8,128)(2,1)} %bitcast.16), calls=%async_computation | async-start | bytes 6291456 | tf_op jit(solution)/shard_map/all_to_all | solution.py:119
  134.0 251.2 %all-gather.5.cloned.1.call-start = ((), (), s32[]{:S(2)}) async-start(), calls=%async_computation.3 | async-start | bytes 4456448 | tf_op jit(solution)/shard_map/all_gather | solution.py:77
  206.7 1.5 collective-permute-start.6
  209.9 73.0 %collective-permute-start.5 = (bf16[1536,1024]{1,0:T(8,128)(2,1)S(1)}, bf16[1536,1024]{1,0:T(8,128)(2,1)S(1)}, u32[]{:S(2)}, u32[]{:S(2)}) collective-permute-start(bf16[1536,1024]{1,0:T(8,128)(2,1)S(1)} %copy-done.1), channel_id=1, source_target_pairs={{0,24},{8,16},{16,8},{24,0},{1,25},{9,17},{17,9},{25,1},{2,26},{10... | collective-permute-start | bytes 9437192 | tf_op jit(solution)/shard_map/ppermute | solution.py:94
  298.4 86.9 %copy-start.5 = (f32[256,4]{0,1:T(4,128)S(1)}, f32[256,4]{0,1:T(4,128)}, u32[]{:S(2)}) copy-start(f32[256,4]{0,1:T(4,128)} %param.17) | copy-start | bytes 12292
  298.4 107.1 %all-to-all-start.1 = ((bf16[32,48,1024]{2,1,0:T(8,128)(2,1)}), bf16[32,48,1024]{2,1,0:T(8,128)(2,1)S(1)}, u32[]{:S(2)}, u32[]{:S(2)}) async-start(bf16[32,48,1024]{2,1,0:T(8,128)(2,1)} %bitcast.69), calls=%async_computation.1 | async-start | bytes 6291456 | tf_op jit(solution)/shard_map/all_to_all | solution.py:130
  385.3 7.4 %collective-permute-start.7 = (bf16[1024,2048]{1,0:T(8,128)(2,1)}, bf16[1024,2048]{1,0:T(8,128)(2,1)S(1)}, u32[]{:S(2)}, u32[]{:S(2)}) collective-permute-start(bf16[1024,2048]{1,0:T(8,128)(2,1)} %all-gather.5.cloned.1.call-done), channel_id=1, source_target_pairs={{0,1},{1,0},{2,3},{3,2},{4,5},{5,4},{6,7},{7,6},{8,9},{9,8},{10,11... | collective-permute-start | bytes 12582920 | tf_op jit(solution)/shard_map/ppermute | solution.py:66
Sparse Core Ops, SparseCore 0:
  10.8 103.0 all-gather.2
  210.0 175.2 all-gather.4

commit v3 on v2

--- a/solution.py
+++ b/solution.py
@@ -74,9 +74,13 @@
         half = shard.shape[1] // 2
         mine = lax.dynamic_slice_in_dim(shard, core * half, half, 1)
         other = swap(lax.dynamic_slice_in_dim(shard, (1 - core) * half, half, 1))
-        return lax.all_gather(ordered(mine, other, 0), PLANE, axis=0, tiled=True)
+        return ordered(mine, other, 0)
 
-    down_half = column_half(latent_down)
+    def gather(half):
+        return lax.all_gather(half, PLANE, axis=0, tiled=True)
+
+    down_half = gather(column_half(latent_down))
+    up_pair = column_half(latent_up)
     partner_tokens = swap(tokens)
 
     blocks = []
@@ -105,8 +109,6 @@
     hit = rows_of[:, :, None] == jnp.arange(row_count, dtype=jnp.int32)[None, None, :]
     spread = jnp.any(hit, axis=1).astype(jnp.bfloat16)
     weight = jnp.sum(jnp.where(hit, combine_weights[:, :, None], 0.0), axis=1)
-    weight_high = weight.astype(jnp.bfloat16)
-    weight_low = (weight - weight_high.astype(jnp.float32)).astype(jnp.bfloat16)
 
     for_partner = dot32(partner_tokens, down_half).astype(jnp.bfloat16)
     from_partner = swap(for_partner)
@@ -117,24 +119,34 @@
     ).astype(jnp.bfloat16)
     outgoing = outgoing.reshape(local_experts * peer_count, slot_width, latent_width)
     arrived = lax.all_to_all(outgoing, ALL, split_axis=0, concat_axis=0, tiled=True)
-    arrived, latent_up = lax.optimization_barrier((arrived, latent_up))
-    rows = arrived.reshape(-1, latent_width)
+    arrived, up_pair, blocks[-1] = lax.optimization_barrier((arrived, up_pair, blocks[-1]))
+    groups = local_experts * peer_count
+    units = expert_down.shape[1]
+    weight = weight.reshape(tok_count, groups, slot_width)
+    cut = slot_width // 2
+    up_half = gather(up_pair)
+    combined = jnp.zeros((tok_count, latent_width), jnp.float32)
+    for low, high in ((0, cut), (cut, slot_width)):
+        rows = arrived[:, low:high].reshape(-1, latent_width)
+        total = jnp.zeros(rows.shape, jnp.float32)
+        for part in blocks:
+            both = dot32(rows, part[:latent_width])
+            hidden = (jax.nn.silu(both[:, :units]) * both[:, units:]).astype(jnp.bfloat16)
+            term = dot32(hidden, part[latent_width:]).astype(jnp.bfloat16)
+            total = total + term.astype(jnp.float32)
+        served = total.astype(jnp.bfloat16).reshape(groups, high - low, latent_width)
+        back = lax.all_to_all(served, ALL, split_axis=0, concat_axis=0, tiled=True)
+        back = back.reshape(-1, latent_width)
+        share = weight[:, :, low:high].reshape(tok_count, -1)
+        share_high = share.astype(jnp.bfloat16)
+        share_low = (share - share_high.astype(jnp.float32)).astype(jnp.bfloat16)
+        combined = combined + dot32(share_high, back) + dot32(share_low, back)
+    combined = combined.astype(jnp.bfloat16)
 
-    total = jnp.zeros((row_count, latent_width), jnp.float32)
-    units = expert_down.shape[1]
-    for part in blocks:
-        both = dot32(rows, part[:latent_width])
-        hidden = (jax.nn.silu(both[:, :units]) * both[:, units:]).astype(jnp.bfloat16)
-        total = total + dot32(hidden, part[latent_width:]).astype(jnp.bfloat16).astype(jnp.float32)
-    served = total.astype(jnp.bfloat16).reshape(local_experts * peer_count, slot_width, latent_width)
-    back = lax.all_to_all(served, ALL, split_axis=0, concat_axis=0, tiled=True)
-    up_half = column_half(latent_up)
-    up_whole = ordered(up_half, swap(up_half), 1)
-    back, up_whole = lax.optimization_barrier((back, up_whole))
-    back = back.reshape(row_count, latent_width)
-    combined = (dot32(weight_high, back) + dot32(weight_low, back)).astype(jnp.bfloat16)
-
-    return dot32(combined, up_whole).astype(jnp.bfloat16)
+    up_other = swap(up_half)
+    mine = dot32(combined, up_half).astype(jnp.bfloat16)
+    other = dot32(combined, up_other).astype(jnp.bfloat16)
+    return ordered(mine, other, 1)
 
 
 def solution(mesh):

time: 425 us -> 409 us (0.962)
  waiting for transfers between devices: 287 us -> 255 us
  matrix products: 60.3 us -> 77.7 us
  other arithmetic: 37.7 us -> 25.4 us
  starting transfers between devices: 14.4 us -> 21.1 us
    all_to_all x1, waiting for transfers between devices: 72.4 us -> 0.01 us  [on_device(): lax.all_to_all(outgoing, ALL, split_axis=0, concat_axis=0, tiled=True)]
    ppermute x3, waiting for transfers between devices: 123 us -> 177 us  [exchange(): return lax.ppermute(blocks[shift], 'dp', pairs)]
    all_gather x2, waiting for transfers between devices: 83.9 us -> 43.1 us  [gather(): return lax.all_gather(half, PLANE, axis=0, tiled=True)]
    all_to_all x1 -> x2, waiting for transfers between devices: 0.01 us -> 32.9 us  [on_device(): back = lax.all_to_all(served, ALL, split_axis=0, concat_axis=0, tiled=True)]
    dot_general x12 -> x24, matrix products: 57.6 us -> 75 us  [dot32(): return jnp.dot(a, b, preferred_element_type=jnp.float32)]
    concatenate x3, other arithmetic: 9.23 us -> 2.98 us  [ordered(): return jnp.concatenate([first, second], axis=axis)]
    all_to_all x1 -> x2, starting transfers between devices: 2.91 us -> 8.11 us  [on_device(): back = lax.all_to_all(served, ALL, split_axis=0, concat_axis=0, tiled=True)]
    ppermute x5, waiting for transfers between devices: 7.59 us -> 2.46 us  [swap(): return lax.ppermute(value, 'core', [(0, 1), (1, 0)])]
  transfers between devices with their start and end apart: 12 -> 13, of which waited for: 7 -> 6; matrix products, arithmetic and copies ran while one was open for 19% -> 23% of each run, Pallas kernels for 0% -> 0%
where the time goes in v3:
time: 409 us; the launch traced here: 408 us
  waiting for transfers between devices  255 us (62%)
  matrix products  77.7 us (19%)
  other arithmetic  25.4 us (6%)
  starting transfers between devices  21.1 us (5%)
  local copies, waits for them, and re-layouts  15.5 us (4%)
  between operations  13.8 us (3%)
    ppermute x3, waiting for transfers between devices, exchange(): return lax.ppermute(blocks[shift], 'dp', pairs)  177 us
    dot_general x24, matrix products, dot32(): return jnp.dot(a, b, preferred_element_type=jnp.float32)  75 us
    all_gather x2, waiting for transfers between devices, gather(): return lax.all_gather(half, PLANE, axis=0, tiled=True)  43.1 us
    all_to_all x2, waiting for transfers between devices, on_device(): back = lax.all_to_all(served, ALL, split_axis=0, concat_axis=0, tiled=True)  32.9 us
    another operation x5, other arithmetic  9.45 us
  transfers between devices with their start and end apart: 13, of which 6 were waited for; matrix products, arithmetic and copies ran while one was open for 23% of the time, Pallas kernels for 0%

profile of v3, /device:TPU:0, one launch (start us, length us, event | category | flops | bytes accessed | tf_op | source)
XLA Modules:
  0.0 408.4 jit_solution(15331054824748588004)
XLA Ops:
  10.7 2.3 dynamic-slice_bitcast_fusion.2
  13.8 4.5 %dynamic-slice_bitcast_fusion = (bf16[1024,512]{1,0:T(8,128)(2,1)}, bf16[1024,512]{1,0:T(8,128)(2,1)S(1)}, bf16[1024,512]{1,0:T(8,128)(2,1)S(1)}, bf16[1024,512]...) fusion(bf16[4,1024,512]{2,1,0:T(8,128)(2,1)S(1)} %copy-done, ...), kind=kLoop, calls=%fused_computation.73 | loop fusion | bytes 16777232 | tf_op jit(solution)/shard_map/jit(dynamic_index_in_dim)/squeeze | solution.py:90
  18.3 2.1 pad_maximum_fusion.1
  20.4 2.8 collective-permute-start.1
  23.3 2.0 pad_maximum_fusion.2
  25.3 1.5 collective-permute-start.2
  27.2 9.0 %reduce-window.15 = s32[32,8,128]{2,1,0:T(8,128)S(1)} reduce-window(s32[32,8,128]{2,1,0:T(8,128)S(1)} %fusion.100, s32[]{:T(128)} %constant.99.clone.1), window={size=1x1x128 pad=0_0x0_0x127_0}, to_apply=%region_0.1 | reduce-window | flops 4161536 | bytes 262148 | tf_op jit(solution)/shard_map/reduce-window
  39.7 1.0 select_reduce_fusion.1
  41.6 2.0 pad_maximum_fusion
  43.6 72.7 %collective-permute-done.1 = bf16[1536,1024]{1,0:T(8,128)(2,1)} collective-permute-done((bf16[1536,1024]{1,0:T(8,128)(2,1)}, bf16[1536,1024]{1,0:T(8,128)(2,1)}, u32[]{:S(2)}, u32[]{:S(2)}) %collective-permute-start.1) | collective-permute-done | bytes 3145760 | tf_op jit(solution)/shard_map/ppermute | solution.py:98
  116.3 4.2 %fusion.56 = bf16[256,512]{0,1:T(8,128)(2,1)S(1)} fusion(bf16[4096,512]{1,0:T(8,128)(2,1)} %all-gather.3.cloned.1.call-done, bf16[256,4096]{1,0:T(8,128)(2,1)} %collective-permute-done.3), kind=kOutput, calls=%fused_computation.70 | convolution fusion | flops 1073872896 | bytes 6553600 | tf_op jit(solution)/shard_map/dot_general | solution.py:12
  120.9 1.2 fusion
  122.1 4.2 %broadcast_select_fusion.3 = (bf16[256,512]{0,1:T(8,128)(2,1)S(1)}, bf16[256,512]{0,1:T(8,128)(2,1)S(1)}) fusion(bf16[256,512]{0,1:T(8,128)(2,1)S(1)} %collective-permute-done.4, pred[]{:T(512)S(6)} %eq.63, bf16[4096,512]{1,0:T(8,128)(2,1)} %all-gather.3.cloned.1.call-done, bf16[256,4096]{1,0:T(8,128)(2,1)} %param.10), kind=kOutput, calls=%fused_computation.115 | convolution fusion | flops 1074135040 | bytes 7077889 | tf_op jit(solution)/shard_map/dot_general | solution.py:12
  126.3 2.7 convolution_convert_fusion
  129.0 4.9 %all-to-all-start = ((bf16[32,48,1024]{2,1,0:T(8,128)(2,1)}), bf16[32,48,1024]{2,1,0:T(8,128)(2,1)S(1)}, u32[]{:S(2)}, u32[]{:S(2)}) async-start(bf16[32,48,1024]{2,1,0:T(8,128)(2,1)} %bitcast.17), calls=%async_computation | async-start | bytes 6291456 | tf_op jit(solution)/shard_map/all_to_all | solution.py:121
  134.1 2.7 collective-permute-start.6
  137.0 1.5 collective-permute-done.5
  140.1 103.9 %collective-permute-done.6 = bf16[1536,1024]{1,0:T(8,128)(2,1)} collective-permute-done((bf16[1536,1024]{1,0:T(8,128)(2,1)}, bf16[1536,1024]{1,0:T(8,128)(2,1)}, u32[]{:S(2)}, u32[]{:S(2)}) %collective-permute-start.6) | collective-permute-done | bytes 3145760 | tf_op jit(solution)/shard_map/ppermute | solution.py:98
  244.0 1.5 fusion.117
  246.1 1.8 fusion.42
  247.9 2.2 convolution_convert_fusion.10
  250.1 3.5 fusion.7
  253.6 3.4 fusion.11
  257.0 3.4 fusion.3
  260.4 2.2 convolution_convert_fusion.8
  262.7 2.2 convolution_convert_fusion.9
  264.9 3.7 add_convert_fusion.1
  268.6 4.3 %all-to-all-start.1 = ((bf16[32,24,1024]{2,1,0:T(8,128)(2,1)}), bf16[32,24,1024]{2,1,0:T(8,128)(2,1)S(1)}, u32[]{:S(2)}, u32[]{:S(2)}) async-start(bf16[32,24,1024]{2,1,0:T(8,128)(2,1)} %bitcast.22), calls=%async_computation.1 | async-start | bytes 3145728 | tf_op jit(solution)/shard_map/all_to_all | solution.py:138
  273.0 3.3 fusion.41
  276.3 3.4 convolution_convert_fusion.6
  279.7 3.4 fusion.5
  283.1 3.4 fusion.9
  286.4 5.0 %fusion.1 = f32[768,1024]{1,0:T(8,128)} fusion(bf16[768,1024]{1,0:T(8,128)(2,1)S(1)} %bitcast.96, bf16[1536,1024]{1,0:T(8,128)(2,1)} %collective-permute-done.6), kind=kOutput, calls=%fused_computation.13 | convolution fusion | flops 1610612736 | bytes 6815744 | tf_op jit(solution)/shard_map/dot_general | solution.py:12
  291.4 3.4 convolution_convert_fusion.4
  294.8 3.6 convolution_convert_fusion.5
  298.4 43.1 %all-gather.5.cloned.1.call-done = bf16[1024,2048]{1,0:T(8,128)(2,1)} async-done(((bf16[64,2048]{1,0:T(8,128)(2,1)}), bf16[1024,2048]{1,0:T(8,128)(2,1)}) %all-gather.5.cloned.1.call-update) | async-done | bytes 4194320 | tf_op jit(solution)/shard_map/all_gather | solution.py:80
  341.5 5.6 %add_convert_fusion = bf16[768,1024]{1,0:T(8,128)(2,1)} fusion(bf16[768,1024]{1,0:T(8,128)(2,1)} %convolution_convert_fusion.4, bf16[768,1024]{1,0:T(8,128)(2,1)} %convolution_convert_fusion.5, bf16[768,1024]{1,0:T(8,128)(2,1)S(1)} %copy-done.13, bf16[1536,1024]{1,0:T(8,128)(2,1)} %collective-permute-done.6, f32[768,1024]{1,0:T(8,128)} %fusion.1), kind=kOutput, calls=%fused_computation.7 | convolution fusion | flops 814743552 | bytes 10485760 | tf_op jit(solution)/shard_map/dot_general | solution.py:12
  347.1 3.8 all-to-all-start.2
  350.9 1.0 select_reduce_fusion
  352.6 1.3 copy-done.2
  353.9 1.4 fusion.29
  355.2 1.4 fusion.49
  356.6 32.9 %all-to-all-done.2 = bf16[32,24,1024]{2,1,0:T(8,128)(2,1)} async-done(((bf16[32,24,1024]{2,1,0:T(8,128)(2,1)}), bf16[32,24,1024]{2,1,0:T(8,128)(2,1)}, u32[]{:S(2)}, u32[]{:S(2)}) %all-to-all-start.2) | async-done | bytes 1572896 | tf_op jit(solution)/shard_map/all_to_all | solution.py:138
  389.5 2.8 fusion.46
  392.3 2.8 fusion.52
  395.1 3.6 convolution_convert_fusion.1
  398.7 1.3 broadcast_select_fusion.1
  400.1 1.5 pad_maximum_fusion.4
  (77 shorter events, 13.3 us)
Async XLA Ops:
  6.5 109.8 %all-gather.3.cloned.1.call-start = ((), (), s32[]{:S(2)}) async-start(), calls=%async_computation.3 | async-start | bytes 4456448 | tf_op jit(solution)/shard_map/all_gather | solution.py:80
  7.5 1.5 collective-permute-start
  10.7 3.1 copy-start
  20.4 95.8 %collective-permute-start.1 = (bf16[1536,1024]{1,0:T(8,128)(2,1)}, bf16[1536,1024]{1,0:T(8,128)(2,1)}, u32[]{:S(2)}, u32[]{:S(2)}) collective-permute-start(bf16[1536,1024]{1,0:T(8,128)(2,1)} %pad_maximum_fusion.1), channel_id=1, source_target_pairs={{0,8},{8,0},{16,24},{24,16},{1,9},{9,1},{17,25},{25,17},{2,10},{10... | collective-permute-start | bytes 9437192 | tf_op jit(solution)/shard_map/ppermute | solution.py:98
  23.3 3.5 copy-start.10
  23.3 13.4 %copy-start.11 = (s32[32]{0:T(128)S(1)}, s32[32]{0:T(128)}, u32[]{:S(2)}) copy-start(s32[32]{0:T(128)} %param.18) | copy-start | bytes 388
  25.3 91.0 %collective-permute-start.2 = (bf16[1536,1024]{1,0:T(8,128)(2,1)}, bf16[1536,1024]{1,0:T(8,128)(2,1)}, u32[]{:S(2)}, u32[]{:S(2)}) collective-permute-start(bf16[1536,1024]{1,0:T(8,128)(2,1)} %pad_maximum_fusion.2), channel_id=1, source_target_pairs={{0,16},{8,24},{16,0},{24,8},{1,17},{9,25},{17,1},{25,9},{2,18},{10... | collective-permute-start | bytes 9437192 | tf_op jit(solution)/shard_map/ppermute | solution.py:98
  26.8 89.5 %collective-permute-start.3 = (bf16[256,4096]{1,0:T(8,128)(2,1)}, bf16[256,4096]{1,0:T(8,128)(2,1)}, u32[]{:S(2)}, u32[]{:S(2)}) collective-permute-start(bf16[256,4096]{1,0:T(8,128)(2,1)} %param.10), channel_id=1, source_target_pairs={{0,1},{1,0},{2,3},{3,2},{4,5},{5,4},{6,7},{7,6},{8,9},{9,8},{10,11... | collective-permute-start | bytes 6291464 | tf_op jit(solution)/shard_map/ppermute | solution.py:66
  43.6 76.9 %copy-start.6 = (s32[256,4]{1,0:T(8,128)S(1)}, s32[256,4]{1,0:T(8,128)}, u32[]{:S(2)}) copy-start(s32[256,4]{1,0:T(8,128)} %reduce_sum.45) | copy-start | bytes 12292
  43.6 76.9 %copy-start.7 = (s32[256,4]{1,0:T(8,128)S(1)}, s32[256,4]{1,0:T(8,128)}, u32[]{:S(2)}) copy-start(s32[256,4]{1,0:T(8,128)} %reduce_sum.47) | copy-start | bytes 12292
  120.5 1.7 collective-permute-start.4
  129.0 7.9 %copy-start.8 = (bf16[32,4096]{1,0:T(8,128)(2,1)S(1)}, bf16[32,4096]{1,0:T(8,128)(2,1)}, u32[]{:S(2)}) copy-start(bf16[32,4096]{1,0:T(8,128)(2,1)} %param.12) | copy-start | bytes 786436
  129.0 115.0 %all-to-all-start = ((bf16[32,48,1024]{2,1,0:T(8,128)(2,1)}), bf16[32,48,1024]{2,1,0:T(8,128)(2,1)S(1)}, u32[]{:S(2)}, u32[]{:S(2)}) async-start(bf16[32,48,1024]{2,1,0:T(8,128)(2,1)} %bitcast.17), calls=%async_computation | async-start | bytes 6291456 | tf_op jit(solution)/shard_map/all_to_all | solution.py:121
  133.9 207.6 %all-gather.5.cloned.1.call-start = ((), (), s32[]{:S(2)}) async-start(), calls=%async_computation.4 | async-start | bytes 4456448 | tf_op jit(solution)/shard_map/all_gather | solution.py:80
  134.1 109.8 %collective-permute-start.6 = (bf16[1536,1024]{1,0:T(8,128)(2,1)}, bf16[1536,1024]{1,0:T(8,128)(2,1)}, u32[]{:S(2)}, u32[]{:S(2)}) collective-permute-start(bf16[1536,1024]{1,0:T(8,128)(2,1)} %pad_maximum_fusion), channel_id=1, source_target_pairs={{0,24},{8,16},{16,8},{24,0},{1,25},{9,17},{17,9},{25,1},{2,26},{10... | collective-permute-start | bytes 9437192 | tf_op jit(solution)/shard_map/ppermute | solution.py:98
  136.9 1.5 collective-permute-start.5
  244.0 1.5 copy-start.4
  244.0 2.1 copy-start.5
  268.6 4.3 %copy-start.3 = (bf16[32,24,1024]{2,1,0:T(8,128)(2,1)S(1)}, bf16[32,24,1024]{2,1,0:T(8,128)(2,1)}, u32[]{:S(2)}) copy-start(bf16[32,24,1024]{2,1,0:T(8,128)(2,1)} %get-tuple-element.34) | copy-start | bytes 4718596
  268.6 78.5 %all-to-all-start.1 = ((bf16[32,24,1024]{2,1,0:T(8,128)(2,1)}), bf16[32,24,1024]{2,1,0:T(8,128)(2,1)S(1)}, u32[]{:S(2)}, u32[]{:S(2)}) async-start(bf16[32,24,1024]{2,1,0:T(8,128)(2,1)} %bitcast.22), calls=%async_computation.1 | async-start | bytes 3145728 | tf_op jit(solution)/shard_map/all_to_all | solution.py:138
  294.8 46.7 %copy-start.13 = (bf16[768,1024]{1,0:T(8,128)(2,1)S(1)}, bf16[768,1024]{1,0:T(8,128)(2,1)}, u32[]{:S(2)}) copy-start(bf16[768,1024]{1,0:T(8,128)(2,1)} %convolution_convert_fusion.6) | copy-start | bytes 4718596
  341.5 53.6 %collective-permute-start.7 = (bf16[1024,2048]{1,0:T(8,128)(2,1)}, bf16[1024,2048]{1,0:T(8,128)(2,1)}, u32[]{:S(2)}, u32[]{:S(2)}) collective-permute-start(bf16[1024,2048]{1,0:T(8,128)(2,1)} %all-gather.5.cloned.1.call-done), channel_id=1, source_target_pairs={{0,1},{1,0},{2,3},{3,2},{4,5},{5,4},{6,7},{7,6},{8,9},{9,8},{10,11... | collective-permute-start | bytes 12582920 | tf_op jit(solution)/shard_map/ppermute | solution.py:66
  347.1 3.8 copy-start.9
  347.1 3.8 copy-start.1
  347.1 42.4 %all-to-all-start.2 = ((bf16[32,24,1024]{2,1,0:T(8,128)(2,1)}), bf16[32,24,1024]{2,1,0:T(8,128)(2,1)}, u32[]{:S(2)}, u32[]{:S(2)}) async-start(bf16[32,24,1024]{2,1,0:T(8,128)(2,1)} %bitcast.26), calls=%async_computation.2 | async-start | bytes 3145728 | tf_op jit(solution)/shard_map/all_to_all | solution.py:138
  352.5 1.4 copy-start.2
  395.1 3.6 copy-start.12
Sparse Core Ops, SparseCore 0:
  10.8 103.0 all-gather.2
  244.1 97.3 all-gather.4

commit v4 on v3

--- a/solution.py
+++ b/solution.py
@@ -101,7 +101,9 @@
     tied = lax.optimization_barrier((down_half, blocks[-1], *[exchange(s) for s in early]))
     down_half, blocks[-1] = tied[:2]
     blocks[1:-1] = tied[2:]
-    blocks[-1] = exchange(team_size - 1)
+    last_pairs = [(d, d ^ (team_size - 1)) for d in range(team_size)]
+    last_in = lax.ppermute(blocks[-1][:latent_width], "dp", last_pairs)
+    last_out = lax.ppermute(blocks[-1][latent_width:], "dp", last_pairs)
 
     rows_of = place_rows(
         chosen_experts, capacity, fallback, local_experts, slot_cap, spill_peer, peer_count
@@ -118,8 +120,11 @@
         spread, latent, (((0,), (0,)), ((), ())), preferred_element_type=jnp.float32
     ).astype(jnp.bfloat16)
     outgoing = outgoing.reshape(local_experts * peer_count, slot_width, latent_width)
+    outgoing, up_pair = lax.optimization_barrier((outgoing, up_pair))
     arrived = lax.all_to_all(outgoing, ALL, split_axis=0, concat_axis=0, tiled=True)
-    arrived, up_pair, blocks[-1] = lax.optimization_barrier((arrived, up_pair, blocks[-1]))
+    arrived, last_in = lax.optimization_barrier((arrived, last_in))
+    halves = [(part[:latent_width], part[latent_width:]) for part in blocks[:-1]]
+    halves.append((last_in, last_out))
     groups = local_experts * peer_count
     units = expert_down.shape[1]
     weight = weight.reshape(tok_count, groups, slot_width)
@@ -129,10 +134,10 @@
     for low, high in ((0, cut), (cut, slot_width)):
         rows = arrived[:, low:high].reshape(-1, latent_width)
         total = jnp.zeros(rows.shape, jnp.float32)
-        for part in blocks:
-            both = dot32(rows, part[:latent_width])
+        for inward, outward in halves:
+            both = dot32(rows, inward)
             hidden = (jax.nn.silu(both[:, :units]) * both[:, units:]).astype(jnp.bfloat16)
-            term = dot32(hidden, part[latent_width:]).astype(jnp.bfloat16)
+            term = dot32(hidden, outward).astype(jnp.bfloat16)
             total = total + term.astype(jnp.float32)
         served = total.astype(jnp.bfloat16).reshape(groups, high - low, latent_width)
         back = lax.all_to_all(served, ALL, split_axis=0, concat_axis=0, tiled=True)

time: 409 us -> 384 us (0.939); the launches traced: 408 us -> 377 us
  waiting for transfers between devices: 255 us -> 227 us
  matrix products: 77.7 us -> 72.4 us
    ppermute x0 -> x2, waiting for transfers between devices: none -> 106 us  [the longest x1 97.4 us: on_device(): last_in = lax.ppermute(blocks[-1][:latent_width], 'dp', last_pairs)]
    ppermute x3 -> x2, waiting for transfers between devices: 177 us -> 72.7 us  [exchange(): return lax.ppermute(blocks[shift], 'dp', pairs)]
    all_gather x2, waiting for transfers between devices: 43.1 us -> 0.02 us  [gather(): return lax.all_gather(half, PLANE, axis=0, tiled=True)]
    all_to_all x2, waiting for transfers between devices: 32.9 us -> 47.7 us  [on_device(): back = lax.all_to_all(served, ALL, split_axis=0, concat_axis=0, tiled=True)]
    dot_general x24, matrix products: 75 us -> 69.8 us  [dot32(): return jnp.dot(a, b, preferred_element_type=jnp.float32)]
  transfers between devices with their start and end apart: 13 -> 14, of which waited for: 6 -> 7; matrix products, arithmetic and copies ran while one was open for 23% -> 26% of each run, Pallas kernels for 0% -> 0%
where the time goes in v4:
time: 384 us; the launch traced here: 377 us
  waiting for transfers between devices  227 us (59%)
  matrix products  72.4 us (19%)
  other arithmetic  23.7 us (6%)
  starting transfers between devices  21.5 us (6%)
  local copies, waits for them, and re-layouts  17.8 us (5%)
  between operations  14.2 us (4%)
    ppermute x1, waiting for transfers between devices, on_device(): last_in = lax.ppermute(blocks[-1][:latent_width], 'dp', last_pairs)  97.4 us
    ppermute x2, waiting for transfers between devices, exchange(): return lax.ppermute(blocks[shift], 'dp', pairs)  72.7 us
    dot_general x24, matrix products, dot32(): return jnp.dot(a, b, preferred_element_type=jnp.float32)  69.8 us
    all_to_all x2, waiting for transfers between devices, on_device(): back = lax.all_to_all(served, ALL, split_axis=0, concat_axis=0, tiled=True)  47.7 us
    another operation x5, other arithmetic  9.46 us
    ppermute x1, waiting for transfers between devices, on_device(): last_out = lax.ppermute(blocks[-1][latent_width:], 'dp', last_pairs)  8.12 us
    squeeze x2, local copies, waits for them, and re-layouts, on_device(): lax.dynamic_index_in_dim(w, partner, 0, keepdims=False)  7.93 us
    all_to_all x2, starting transfers between devices, on_device(): back = lax.all_to_all(served, ALL, split_axis=0, concat_axis=0, tiled=True)  7.77 us
  transfers between devices with their start and end apart: 14, of which 7 were waited for; matrix products, arithmetic and copies ran while one was open for 26% of the time, Pallas kernels for 0%

profile of v4, /device:TPU:0, one launch (start us, length us, event | category | flops | bytes accessed | tf_op | source)
XLA Modules:
  0.0 376.8 jit_solution(15368083515423809081)
XLA Ops:
  10.7 3.3 dynamic-slice_bitcast_fusion.2
  14.0 4.6 %dynamic-slice_bitcast_fusion = (bf16[1024,512]{1,0:T(8,128)(2,1)}, bf16[1024,512]{1,0:T(8,128)(2,1)S(1)}, bf16[1024,512]{1,0:T(8,128)(2,1)}, bf16[1024,512]{1,0...) fusion(bf16[4,1024,512]{2,1,0:T(8,128)(2,1)S(1)} %copy-done, ...), kind=kLoop, calls=%fused_computation.69 | loop fusion | bytes 16777232 | tf_op jit(solution)/shard_map/jit(dynamic_index_in_dim)/squeeze | solution.py:90
  18.6 2.1 pad_maximum_fusion.1
  20.8 2.8 collective-permute-start.1
  23.6 2.0 pad_maximum_fusion.2
  25.6 1.5 collective-permute-start.2
  28.7 9.0 %reduce-window.15 = s32[32,8,128]{2,1,0:T(8,128)S(1)} reduce-window(s32[32,8,128]{2,1,0:T(8,128)S(1)} %fusion.94, s32[]{:T(128)} %constant.99.clone.1), window={size=1x1x128 pad=0_0x0_0x127_0}, to_apply=%region_0.1 | reduce-window | flops 4161536 | bytes 262148 | tf_op jit(solution)/shard_map/reduce-window
  40.3 1.2 fusion
  41.5 2.2 pad_maximum_fusion
  43.7 72.7 %collective-permute-done.1 = bf16[1536,1024]{1,0:T(8,128)(2,1)} collective-permute-done((bf16[1536,1024]{1,0:T(8,128)(2,1)}, bf16[1536,1024]{1,0:T(8,128)(2,1)}, u32[]{:S(2)}, u32[]{:S(2)}) %collective-permute-start.1) | collective-permute-done | bytes 3145760 | tf_op jit(solution)/shard_map/ppermute | solution.py:98
  116.4 4.9 %fusion.52 = bf16[256,512]{0,1:T(8,128)(2,1)} fusion(bf16[4096,512]{1,0:T(8,128)(2,1)} %all-gather.3.cloned.1.call-done, bf16[256,4096]{1,0:T(8,128)(2,1)} %collective-permute-done.3), kind=kOutput, calls=%fused_computation.66 | convolution fusion | flops 1073872896 | bytes 6553600 | tf_op jit(solution)/shard_map/dot_general | solution.py:12
  123.2 4.1 %broadcast_select_fusion.3 = (bf16[256,512]{0,1:T(8,128)(2,1)S(1)}, bf16[256,512]{0,1:T(8,128)(2,1)S(1)}) fusion(bf16[256,512]{0,1:T(8,128)(2,1)} %collective-permute-done.4, pred[]{:T(512)S(6)} %eq.63, bf16[4096,512]{1,0:T(8,128)(2,1)} %all-gather.3.cloned.1.call-done, bf16[256,4096]{1,0:T(8,128)(2,1)} %param.10), kind=kOutput, calls=%fused_computation.109 | convolution fusion | flops 1074135040 | bytes 7077889 | tf_op jit(solution)/shard_map/dot_general | solution.py:12
  127.3 2.6 convolution_convert_fusion
  130.0 4.8 %all-to-all-start = ((bf16[32,48,1024]{2,1,0:T(8,128)(2,1)}), bf16[32,48,1024]{2,1,0:T(8,128)(2,1)}, u32[]{:S(2)}, u32[]{:S(2)}) async-start(bf16[32,48,1024]{2,1,0:T(8,128)(2,1)} %bitcast.17), calls=%async_computation | async-start | bytes 6291456 | tf_op jit(solution)/shard_map/all_to_all | solution.py:124
  135.0 1.5 slice.96
  136.5 2.6 collective-permute-start.6
  139.1 1.1 slice.110
  140.5 97.4 %collective-permute-done.6 = bf16[1024,1024]{1,0:T(8,128)(2,1)} collective-permute-done((bf16[1024,1024]{1,0:T(8,128)(2,1)}, bf16[1024,1024]{1,0:T(8,128)(2,1)}, u32[]{:S(2)}, u32[]{:S(2)}) %collective-permute-start.6) | collective-permute-done | bytes 2097184 | tf_op jit(solution)/shard_map/ppermute | solution.py:105
  238.0 2.2 fusion.111
  240.2 3.0 fusion.38
  243.2 3.4 fusion.3
  246.6 3.4 fusion.7
  250.0 3.4 fusion.113
  253.4 2.2 convolution_convert_fusion.10
  255.7 2.2 convolution_convert_fusion.8
  257.9 2.2 convolution_convert_fusion.9
  260.2 8.1 %collective-permute-done.7 = bf16[512,1024]{1,0:T(8,128)(2,1)} collective-permute-done((bf16[512,1024]{1,0:T(8,128)(2,1)}, bf16[512,1024]{1,0:T(8,128)(2,1)}, u32[]{:S(2)}, u32[]{:S(2)}) %collective-permute-start.7) | collective-permute-done | bytes 1048608 | tf_op jit(solution)/shard_map/ppermute | solution.py:106
  268.3 3.7 add_convert_fusion.1
  272.0 4.1 %all-to-all-start.1 = ((bf16[32,24,1024]{2,1,0:T(8,128)(2,1)}), bf16[32,24,1024]{2,1,0:T(8,128)(2,1)S(1)}, u32[]{:S(2)}, u32[]{:S(2)}) async-start(bf16[32,24,1024]{2,1,0:T(8,128)(2,1)} %bitcast.22), calls=%async_computation.1 | async-start | bytes 3145728 | tf_op jit(solution)/shard_map/all_to_all | solution.py:143
  276.1 3.3 fusion.37
  279.4 2.2 convolution_convert_fusion.6
  281.6 3.4 fusion.1
  285.0 3.4 fusion.5
  288.4 3.4 fusion.114
  291.8 2.2 convolution_convert_fusion.4
  294.0 2.2 convolution_convert_fusion.5
  296.3 3.7 add_convert_fusion
  300.0 14.9 %all-to-all-done.1 = bf16[32,24,1024]{2,1,0:T(8,128)(2,1)S(1)} async-done(((bf16[32,24,1024]{2,1,0:T(8,128)(2,1)}), bf16[32,24,1024]{2,1,0:T(8,128)(2,1)S(1)}, u32[]{:S(2)}, u32[]{:S(2)}) %all-to-all-start.1) | async-done | bytes 1572896 | tf_op jit(solution)/shard_map/all_to_all | solution.py:143
  314.9 3.7 all-to-all-start.2
  320.6 1.3 copy-done.2
  321.9 1.4 fusion.25
  323.2 1.4 fusion.45
  324.6 32.8 %all-to-all-done.2 = bf16[32,24,1024]{2,1,0:T(8,128)(2,1)} async-done(((bf16[32,24,1024]{2,1,0:T(8,128)(2,1)}), bf16[32,24,1024]{2,1,0:T(8,128)(2,1)}, u32[]{:S(2)}, u32[]{:S(2)}) %all-to-all-start.2) | async-done | bytes 1572896 | tf_op jit(solution)/shard_map/all_to_all | solution.py:143
  357.4 2.8 fusion.42
  360.2 2.9 fusion.48
  363.2 1.3 convolution_convert_fusion.2
  364.5 3.5 broadcast_select_fusion.1
  368.0 1.5 pad_maximum_fusion.4
  (75 shorter events, 12.5 us)
Async XLA Ops:
  6.5 109.9 %all-gather.3.cloned.1.call-start = ((), (), s32[]{:S(2)}) async-start(), calls=%async_computation.3 | async-start | bytes 4456448 | tf_op jit(solution)/shard_map/all_gather | solution.py:80
  7.5 1.5 collective-permute-start
  10.7 3.3 copy-start
  20.8 95.6 %collective-permute-start.1 = (bf16[1536,1024]{1,0:T(8,128)(2,1)}, bf16[1536,1024]{1,0:T(8,128)(2,1)}, u32[]{:S(2)}, u32[]{:S(2)}) collective-permute-start(bf16[1536,1024]{1,0:T(8,128)(2,1)} %pad_maximum_fusion.1), channel_id=1, source_target_pairs={{0,8},{8,0},{16,24},{24,16},{1,9},{9,1},{17,25},{25,17},{2,10},{10... | collective-permute-start | bytes 9437192 | tf_op jit(solution)/shard_map/ppermute | solution.py:98
  23.6 3.5 copy-start.4
  23.6 4.7 %copy-start.7 = (s32[256,4]{0,1:T(4,128)S(1)}, s32[256,4]{0,1:T(4,128)}, u32[]{:S(2)}) copy-start(s32[256,4]{0,1:T(4,128)} %param.16) | copy-start | bytes 12292
  23.6 14.5 %copy-start.8 = (s32[32]{0:T(128)S(1)}, s32[32]{0:T(128)}, u32[]{:S(2)}) copy-start(s32[32]{0:T(128)} %param.18) | copy-start | bytes 388
  25.6 13.7 %copy-start.9 = (s32[1,128]{1,0:T(1,128)S(1)}, s32[1,128]{1,0:T(1,128)}, u32[]{:S(2)}) copy-start(s32[1,128]{1,0:T(1,128)} %param.19) | copy-start | bytes 1540
  25.6 90.8 %collective-permute-start.2 = (bf16[1536,1024]{1,0:T(8,128)(2,1)}, bf16[1536,1024]{1,0:T(8,128)(2,1)}, u32[]{:S(2)}, u32[]{:S(2)}) collective-permute-start(bf16[1536,1024]{1,0:T(8,128)(2,1)} %pad_maximum_fusion.2), channel_id=1, source_target_pairs={{0,16},{8,24},{16,0},{24,8},{1,17},{9,25},{17,1},{25,9},{2,18},{10... | collective-permute-start | bytes 9437192 | tf_op jit(solution)/shard_map/ppermute | solution.py:98
  27.1 89.3 %collective-permute-start.3 = (bf16[256,4096]{1,0:T(8,128)(2,1)}, bf16[256,4096]{1,0:T(8,128)(2,1)}, u32[]{:S(2)}, u32[]{:S(2)}) collective-permute-start(bf16[256,4096]{1,0:T(8,128)(2,1)} %param.10), channel_id=1, source_target_pairs={{0,1},{1,0},{2,3},{3,2},{4,5},{5,4},{6,7},{7,6},{8,9},{9,8},{10,11... | collective-permute-start | bytes 6291464 | tf_op jit(solution)/shard_map/ppermute | solution.py:66
  27.8 93.6 %collective-permute-start.5 = (bf16[32,2048]{1,0:T(8,128)(2,1)}, bf16[32,2048]{1,0:T(8,128)(2,1)}, u32[]{:S(2)}, u32[]{:S(2)}) collective-permute-start(bf16[32,2048]{1,0:T(8,128)(2,1)} %constant_dynamic-slice_fusion), channel_id=1, source_target_pairs={{0,1},{1,0},{2,3},{3,2},{4,5},{5,4},{6,7},{7,6},{8,9},{9,8},{10,11... | collective-permute-start | bytes 393224 | tf_op jit(solution)/shard_map/ppermute | solution.py:66
  116.4 5.0 %copy-start.5 = (bf16[32,4096]{1,0:T(8,128)(2,1)S(1)}, bf16[32,4096]{1,0:T(8,128)(2,1)}, u32[]{:S(2)}) copy-start(bf16[32,4096]{1,0:T(8,128)(2,1)} %param.12) | copy-start | bytes 786436
  121.3 1.9 collective-permute-start.4
  130.0 108.0 %all-to-all-start = ((bf16[32,48,1024]{2,1,0:T(8,128)(2,1)}), bf16[32,48,1024]{2,1,0:T(8,128)(2,1)}, u32[]{:S(2)}, u32[]{:S(2)}) async-start(bf16[32,48,1024]{2,1,0:T(8,128)(2,1)} %bitcast.17), calls=%async_computation | async-start | bytes 6291456 | tf_op jit(solution)/shard_map/all_to_all | solution.py:124
  134.8 183.8 %all-gather.5.cloned.1.call-start = ((), (), s32[]{:S(2)}) async-start(), calls=%async_computation.4 | async-start | bytes 4456448 | tf_op jit(solution)/shard_map/all_gather | solution.py:80
  136.5 101.4 %collective-permute-start.6 = (bf16[1024,1024]{1,0:T(8,128)(2,1)}, bf16[1024,1024]{1,0:T(8,128)(2,1)}, u32[]{:S(2)}, u32[]{:S(2)}) collective-permute-start(bf16[1024,1024]{1,0:T(8,128)(2,1)} %slice.96), channel_id=1, source_target_pairs={{0,24},{8,16},{16,8},{24,0},{1,25},{9,17},{17,9},{25,1},{2,26},{10... | collective-permute-start | bytes 6291464 | tf_op jit(solution)/shard_map/ppermute | solution.py:105
  140.2 128.1 %collective-permute-start.7 = (bf16[512,1024]{1,0:T(8,128)(2,1)}, bf16[512,1024]{1,0:T(8,128)(2,1)}, u32[]{:S(2)}, u32[]{:S(2)}) collective-permute-start(bf16[512,1024]{1,0:T(8,128)(2,1)} %slice.110), channel_id=1, source_target_pairs={{0,24},{8,16},{16,8},{24,0},{1,25},{9,17},{17,9},{25,1},{2,26},{10... | collective-permute-start | bytes 3145736 | tf_op jit(solution)/shard_map/ppermute | solution.py:106
  140.5 99.6 %copy-start.3 = (bf16[1024,512]{1,0:T(8,128)(2,1)S(1)}, bf16[1024,512]{1,0:T(8,128)(2,1)}, u32[]{:S(2)}) copy-start(bf16[1024,512]{1,0:T(8,128)(2,1)} %get-tuple-element.29) | copy-start | bytes 3145732
  272.0 43.0 %all-to-all-start.1 = ((bf16[32,24,1024]{2,1,0:T(8,128)(2,1)}), bf16[32,24,1024]{2,1,0:T(8,128)(2,1)S(1)}, u32[]{:S(2)}, u32[]{:S(2)}) async-start(bf16[32,24,1024]{2,1,0:T(8,128)(2,1)} %bitcast.22), calls=%async_computation.1 | async-start | bytes 3145728 | tf_op jit(solution)/shard_map/all_to_all | solution.py:143
  300.0 18.9 %copy-start.6 = (f32[256,4]{0,1:T(4,128)S(1)}, f32[256,4]{0,1:T(4,128)}, u32[]{:S(2)}) copy-start(f32[256,4]{0,1:T(4,128)} %param.17) | copy-start | bytes 12292
  314.9 4.0 %copy-start.1 = (bf16[32,24,1024]{2,1,0:T(8,128)(2,1)}, bf16[32,24,1024]{2,1,0:T(8,128)(2,1)S(1)}, u32[]{:S(2)}) copy-start(bf16[32,24,1024]{2,1,0:T(8,128)(2,1)S(1)} %all-to-all-done.1) | copy-start | bytes 4718596
  314.9 42.5 %all-to-all-start.2 = ((bf16[32,24,1024]{2,1,0:T(8,128)(2,1)}), bf16[32,24,1024]{2,1,0:T(8,128)(2,1)}, u32[]{:S(2)}, u32[]{:S(2)}) async-start(bf16[32,24,1024]{2,1,0:T(8,128)(2,1)} %bitcast.26), calls=%async_computation.2 | async-start | bytes 3145728 | tf_op jit(solution)/shard_map/all_to_all | solution.py:143
  318.6 45.8 %collective-permute-start.8 = (bf16[1024,2048]{1,0:T(8,128)(2,1)}, bf16[1024,2048]{1,0:T(8,128)(2,1)}, u32[]{:S(2)}, u32[]{:S(2)}) collective-permute-start(bf16[1024,2048]{1,0:T(8,128)(2,1)} %all-gather.5.cloned.1.call-done), channel_id=1, source_target_pairs={{0,1},{1,0},{2,3},{3,2},{4,5},{5,4},{6,7},{7,6},{8,9},{9,8},{10,11... | collective-permute-start | bytes 12582920 | tf_op jit(solution)/shard_map/ppermute | solution.py:66
  320.4 1.4 copy-start.2
  360.2 2.9 copy-start.10
Sparse Core Ops, SparseCore 0:
  10.8 102.9 all-gather.2
  140.7 123.4 all-gather.4
